TPU v7x, 256 devices: a whole 4x4x8 slice. The times are simulated.
256 devices in a mesh: tile: 64 (over x, y_hi, z), slot: 4 (over y_lo, core).
Axes of the slice: x: 4, y: 4 (y_hi: 2, y_lo: 2; y = y_hi * 2 + y_lo), z: 8, core: 2. Of those that a mesh axis runs over, the one named last changes fastest.
Arguments:
- queries: bfloat16 [64, 192, 2560], P('tile', None, 'slot'), may hold values from -5 to 5
- current_keys: bfloat16 [64, 192, 2560], P('tile', None, 'slot'), may hold values from -5 to 5
- current_values: bfloat16 [64, 192, 2560], P('tile', None, 'slot'), may hold values from -5 to 5
- cache_keys: bfloat16 [4, 64, 192, 2560], P('slot', 'tile'), may hold values from -5 to 5
- cache_values: bfloat16 [4, 64, 192, 2560], P('slot', 'tile'), may hold values from -5 to 5
- slot_order: int32 [4], replicated, may hold values from 0 to 3, each once
- tile_mask: int32 [64, 9], P('tile'), may hold values 0 or 1
- window_reach: int32 [64, 2], P('tile'), may hold values from 1 to 4
Outputs:
- attended: bfloat16 [64, 192, 2560], P('tile', None, 'slot')
Inputs may be any that keep to these rules, and one draw needn't show every extreme that they name: slot_order[c] is the age of the stretch in slot c, 0 the most recent; each age once.
All inputs are finite; a program needn't handle non-finite values. No bound on the sum of `tile_mask` on one device may be relied on, other than what follows from the above.
Results may differ from a plain program's by a relative error of at most 0.0072.
Values may be sent and summed in bfloat16 or wider, within the bound.
A program may use at most 128 MiB of HBM per device.

v0:
```python
import math

import jax
import jax.numpy as jnp
from jax import lax
from jax.sharding import PartitionSpec as P

TH = 8
TW = 8
F = 3
HALO = 4
GX = 8
HD = 128
PAIRS = 22
TOKT = 192


def passed_along(x, axis, by):
    devices = lax.axis_size(axis)
    pairs = [(i, i + by) for i in range(devices) if 0 <= i + by < devices]
    return lax.ppermute(x, axis, pairs)


def rotate_pairs(matrix, moments):
    heads_count = matrix.shape[-1] // HD
    shaped = matrix.reshape(matrix.shape[:-1] + (heads_count, HD))
    frequency = 10000.0 ** (-jnp.arange(PAIRS, dtype=jnp.float32) / PAIRS)
    angles = moments[..., None, None] * frequency
    cosine = jnp.cos(angles)
    sine = jnp.sin(angles)
    first_half = shaped[..., :PAIRS]
    second_half = shaped[..., PAIRS : 2 * PAIRS]
    turned = jnp.concatenate(
        [
            first_half * cosine - second_half * sine,
            first_half * sine + second_half * cosine,
            shaped[..., 2 * PAIRS :],
        ],
        axis=-1,
    )
    return turned.reshape(matrix.shape)


def window_mask(row_tile, col_tile, rows_tiles, bits, reach_rows, reach_cols):
    extent_rows = jnp.arange(TH + 2 * HALO, dtype=jnp.int32)
    offset_rows = extent_rows - HALO
    step_rows = jnp.where(extent_rows < HALO, -1, jnp.where(extent_rows >= TH + HALO, 1, 0))
    rows_good = (
        (offset_rows >= -reach_rows)
        & (offset_rows < TH + reach_rows)
        & (row_tile + step_rows >= 0)
        & (row_tile + step_rows < rows_tiles)
    )
    extent_cols = jnp.arange(TW + 2 * HALO, dtype=jnp.int32)
    offset_cols = extent_cols - HALO
    step_cols = jnp.where(extent_cols < HALO, -1, jnp.where(extent_cols >= TW + HALO, 1, 0))
    cols_good = (
        (offset_cols >= -reach_cols)
        & (offset_cols < TW + reach_cols)
        & (col_tile + step_cols >= 0)
        & (col_tile + step_cols < GX)
    )
    neighbour = (step_rows[:, None] + 1) * 3 + (step_cols[None, :] + 1)
    indices = jnp.arange(9, dtype=jnp.int32)
    forced = jnp.where(indices == 4, 1, bits)
    chosen = jnp.sum(jnp.where(neighbour[..., None] == indices, forced, 0), axis=-1)
    grid_good = rows_good[:, None] & cols_good[None, :] & (chosen > 0)
    return jnp.broadcast_to(grid_good, (F,) + grid_good.shape).reshape(-1)


def attend_blocks(rotated, block_keys, block_values, allowed):
    scaling = 1.0 / math.sqrt(HD)
    for number in range(block_keys.shape[0]):
        scores = (
            jnp.einsum(
                "qhd,khd->hqk", rotated, block_keys[number], preferred_element_type=jnp.float32
            )
            * scaling
        )
        scores = jnp.where(allowed, scores, -jnp.inf)
        highest = jnp.max(scores, axis=-1)
        if number == 0:
            newest = highest
        else:
            newest = jnp.maximum(running, highest)
        weights = jnp.exp(scores - newest[..., None]).astype(jnp.bfloat16)
        product = jnp.einsum(
            "hqk,khd->hqd", weights, block_values[number], preferred_element_type=jnp.float32
        )
        partial_total = jnp.sum(weights.astype(jnp.float32), axis=-1)
        if number == 0:
            total = partial_total
            summed = product
        else:
            factor = jnp.exp(running - newest)
            total = total * factor + partial_total
            summed = summed * factor[..., None] + product
        running = newest
    result = summed / total[..., None]
    return jnp.transpose(result, (1, 0, 2)).reshape(rotated.shape[0], -1).astype(jnp.bfloat16)


def rim_span(direction, length):
    if direction < 0:
        return (length - HALO, HALO)
    if direction > 0:
        return (0, HALO)
    return (0, length)


def neighbour_piece(keys_part, values_part, offset):
    return passed_along((keys_part, values_part), "tile", offset)


def direct_halo(keys_grid, values_grid):
    rows_keys = []
    rows_values = []
    for step_row in (-1, 0, 1):
        band_keys = []
        band_values = []
        for step_col in (-1, 0, 1):
            if step_row == 0 and step_col == 0:
                band_keys.append(keys_grid)
                band_values.append(values_grid)
            else:
                row_start, row_length = rim_span(step_row, TH)
                col_start, col_length = rim_span(step_col, TW)
                part_keys = lax.slice_in_dim(
                    lax.slice_in_dim(keys_grid, row_start, row_start + row_length, axis=2),
                    col_start,
                    col_start + col_length,
                    axis=3,
                )
                part_values = lax.slice_in_dim(
                    lax.slice_in_dim(values_grid, row_start, row_start + row_length, axis=2),
                    col_start,
                    col_start + col_length,
                    axis=3,
                )
                got_keys, got_values = neighbour_piece(
                    part_keys, part_values, -(step_row * GX + step_col)
                )
                band_keys.append(got_keys)
                band_values.append(got_values)
        rows_keys.append(jnp.concatenate(band_keys, axis=3))
        rows_values.append(jnp.concatenate(band_values, axis=3))
    return (jnp.concatenate(rows_keys, axis=2), jnp.concatenate(rows_values, axis=2))


def on_device(
    queries,
    current_keys,
    current_values,
    cache_keys,
    cache_values,
    slot_order,
    tile_mask,
    window_reach,
):
    head_dev = queries.shape[2] // HD
    frames = jnp.arange(TOKT, dtype=jnp.int32) // (TH * TW)
    stretch_count = slot_order.shape[0]
    present = (stretch_count * F + frames).astype(jnp.float32)
    slot_here = lax.axis_index("slot")
    age_here = jnp.sum(
        jnp.where(jnp.arange(stretch_count, dtype=jnp.int32) == slot_here, slot_order, 0)
    )
    moments = ((stretch_count - 1 - age_here) * F + frames).astype(jnp.float32)
    cache_turned = rotate_pairs(cache_keys[0].astype(jnp.float32), moments).astype(jnp.bfloat16)
    slot_keys, slot_values = (
        lax.all_to_all(cache_turned, "slot", split_axis=2, concat_axis=0, tiled=True),
        lax.all_to_all(cache_values[0], "slot", split_axis=2, concat_axis=0, tiled=True),
    )
    now_keys = rotate_pairs(current_keys.astype(jnp.float32), present).astype(jnp.bfloat16)
    stacked_keys = jnp.concatenate([now_keys, slot_keys], axis=0)
    stacked_values = jnp.concatenate([current_values, slot_values], axis=0)
    block_count = stacked_keys.shape[0]
    grid_shape = (block_count, F, TH, TW, stacked_keys.shape[2])
    keys_grid = stacked_keys.reshape(grid_shape)
    values_grid = stacked_values.reshape(grid_shape)
    wide_keys, wide_values = direct_halo(keys_grid, values_grid)
    wide_keys = wide_keys.reshape(block_count, -1, head_dev, HD)
    wide_values = wide_values.reshape(block_count, -1, head_dev, HD)
    tile_here = lax.axis_index("tile")
    rows_tiles = lax.axis_size("tile") // GX
    allowed = window_mask(
        tile_here // GX,
        tile_here % GX,
        rows_tiles,
        tile_mask[0],
        window_reach[0, 0],
        window_reach[0, 1],
    )
    rotated = (
        rotate_pairs(queries[0].astype(jnp.float32), present)
        .astype(jnp.bfloat16)
        .reshape(TOKT, head_dev, HD)
    )
    attended = attend_blocks(rotated, wide_keys, wide_values, allowed)
    return attended[None]


def solution(mesh):
    placed = (
        P("tile", None, "slot"),
        P("tile", None, "slot"),
        P("tile", None, "slot"),
        P("slot", "tile", None, None),
        P("slot", "tile", None, None),
        P(),
        P("tile", None),
        P("tile", None),
    )
    return jax.shard_map(
        on_device, mesh=mesh, in_specs=placed, out_specs=P("tile", None, "slot"), check_vma=False
    )
```

profile of v0, /device:TPU:2, one launch (start us, length us, event | category | flops | bytes accessed | tf_op | source)
XLA Modules:
  0.0 315.5 jit_solution(7635263732105686597)
XLA Ops:
  0.0 5.7 %copy.118 = bf16[1,192,2560]{1,0,2:T(2,128)(2,1)S(1)} copy(bf16[1,192,2560]{2,1,0:T(8,128)(2,1)} %bitcast.177) | data formatting | bytes 1966080 | tf_op jit(solution)/shard_map/squeeze | solution.py:172
  6.3 15.5 %reduce = bf16[2560,192]{1,0:T(8,128)(2,1)} reduce(bf16[2560,1,192]{2,1,0:T(2,128)(2,1)S(1)} %bitcast.165, bf16[]{:T(256)} %broadcast.415), dimensions={1}, to_apply=%bitcast.140.reduce_sub_computation | reduce | bytes 1966082
  21.8 4.2 %reshape.479 = bf16[4,2,61440]{2,1,0:T(2,128)(2,1)} reshape(bf16[2560,192]{1,0:T(8,128)(2,1)} %reduce) | data formatting | bytes 1966080
  26.0 4.8 %all-to-all-start.1 = ((bf16[4,2,61440]{2,1,0:T(2,128)(2,1)}), bf16[4,2,61440]{2,1,0:T(2,128)(2,1)}, u32[]{:S(2)}, u32[]{:S(2)}) async-start(bf16[4,2,61440]{2,1,0:T(2,128)(2,1)} %reshape.479), calls=%async_computation.1 | async-start | bytes 1966080 | tf_op jit(solution)/shard_map/all_to_all | solution.py:172
  38.5 1.4 slice.185
  47.2 1.4 convert_element_type.128
  48.6 5.7 %copy.114 = bf16[1,192,2560]{1,0,2:T(2,128)(2,1)S(1)} copy(bf16[1,192,2560]{2,1,0:T(8,128)(2,1)} %convert_element_type.128) | data formatting | bytes 1966080 | tf_op jit(solution)/shard_map/convert_element_type | solution.py:169
  54.3 15.5 %reduce.1 = bf16[2560,192]{1,0:T(8,128)(2,1)} reduce(bf16[2560,1,192]{2,1,0:T(2,128)(2,1)S(1)} %bitcast.166, bf16[]{:T(256)} %broadcast.415), dimensions={1}, to_apply=%bitcast.142.reduce_sub_computation | reduce | bytes 1966082
  69.8 4.2 %reshape.481 = bf16[4,2,61440]{2,1,0:T(2,128)(2,1)} reshape(bf16[2560,192]{1,0:T(8,128)(2,1)} %reduce.1) | data formatting | bytes 1966080
  74.2 3.5 %all-to-all-start = ((bf16[4,2,61440]{2,1,0:T(2,128)(2,1)}), bf16[4,2,61440]{2,1,0:T(2,128)(2,1)S(1)}, u32[]{:S(2)}, u32[]{:S(2)}) async-start(bf16[4,2,61440]{2,1,0:T(2,128)(2,1)} %reshape.481), calls=%async_computation | async-start | bytes 1966080 | tf_op jit(solution)/shard_map/all_to_all | solution.py:171
  78.8 4.4 %reshape.480 = bf16[2560,1,192]{2,1,0:T(2,128)(2,1)} reshape(bf16[4,2,61440]{2,1,0:T(2,128)(2,1)} %all-to-all-done.1) | data formatting | bytes 1966080
  83.3 5.2 %copy.119 = bf16[1,192,2560]{2,1,0:T(8,128)(2,1)S(1)} copy(bf16[1,192,2560]{1,0,2:T(2,128)(2,1)} %bitcast.163) | data formatting | bytes 1966080 | tf_op jit(solution)/shard_map/all_to_all | solution.py:172
  91.0 1.4 fusion.34
  92.4 7.7 %collective-permute-start.15 = (bf16[5,3,4,4,640]{4,3,2,1,0:T(4,128)(2,1)}, bf16[5,3,4,4,640]{4,3,2,1,0:T(4,128)(2,1)}, u32[]{:S(2)}, u32[]{:S(2)}) collective-permute-start(bf16[5,3,4,4,640]{4,3,2,1,0:T(4,128)(2,1)} %get-tuple-element.47), channel_id=1, source_target_pairs={{36,0},{40,4},{44,8},{48,12},{52,16},{56,20},{60,24},{64,28},{68,3... | collective-permute-start | bytes 921608 | tf_op jit(solution)/shard_map/ppermute | solution.py:21
  100.2 2.2 collective-permute-start.13
  102.4 5.3 %collective-permute-start.10 = (bf16[5,3,4,4,640]{4,3,2,1,0:T(4,128)(2,1)}, bf16[5,3,4,4,640]{4,3,2,1,0:T(4,128)(2,1)}, u32[]{:S(2)}, u32[]{:S(2)}) collective-permute-start(bf16[5,3,4,4,640]{4,3,2,1,0:T(4,128)(2,1)} %get-tuple-element.45), channel_id=1, source_target_pairs={{0,28},{4,32},{8,36},{12,40},{16,44},{20,48},{24,52},{28,56},{32,6... | collective-permute-start | bytes 921608 | tf_op jit(solution)/shard_map/ppermute | solution.py:21
  107.7 14.9 %collective-permute-start.8 = (bf16[5,3,4,4,640]{4,3,2,1,0:T(4,128)(2,1)}, bf16[5,3,4,4,640]{4,3,2,1,0:T(4,128)(2,1)}, u32[]{:S(2)}, u32[]{:S(2)}) collective-permute-start(bf16[5,3,4,4,640]{4,3,2,1,0:T(4,128)(2,1)} %get-tuple-element.44), channel_id=1, source_target_pairs={{0,36},{4,40},{8,44},{12,48},{16,52},{20,56},{24,60},{28,64},{32,6... | collective-permute-start | bytes 921608 | tf_op jit(solution)/shard_map/ppermute | solution.py:21
  122.6 3.0 reshape.482
  125.6 6.0 %copy.115 = bf16[1,192,2560]{2,1,0:T(8,128)(2,1)} copy(bf16[1,192,2560]{1,0,2:T(2,128)(2,1)} %bitcast.164) | data formatting | bytes 1966080 | tf_op jit(solution)/shard_map/all_to_all | solution.py:171
  131.7 1.9 all_to_all.23
  133.8 1.4 fusion.58
  135.2 4.9 %collective-permute-start.7 = (bf16[5,3,4,4,640]{4,3,2,1,0:T(4,128)(2,1)}, bf16[5,3,4,4,640]{4,3,2,1,0:T(4,128)(2,1)}, u32[]{:S(2)}, u32[]{:S(2)}) collective-permute-start(bf16[5,3,4,4,640]{4,3,2,1,0:T(4,128)(2,1)} %get-tuple-element.37), channel_id=1, source_target_pairs={{36,0},{40,4},{44,8},{48,12},{52,16},{56,20},{60,24},{64,28},{68,3... | collective-permute-start | bytes 921608 | tf_op jit(solution)/shard_map/ppermute | solution.py:21
  141.3 1.7 fusion.32
  143.0 2.0 collective-permute-start.14
  145.1 7.2 %collective-permute-start.12 = (bf16[5,3,8,4,640]{4,3,2,1,0:T(4,128)(2,1)}, bf16[5,3,8,4,640]{4,3,2,1,0:T(4,128)(2,1)}, u32[]{:S(2)}, u32[]{:S(2)}) collective-permute-start(bf16[5,3,8,4,640]{4,3,2,1,0:T(4,128)(2,1)} %get-tuple-element.51), channel_id=1, source_target_pairs={{4,0},{8,4},{12,8},{16,12},{20,16},{24,20},{28,24},{32,28},{36,32}... | collective-permute-start | bytes 1843208 | tf_op jit(solution)/shard_map/ppermute | solution.py:21
  152.3 1.9 collective-permute-start.11
  154.2 5.4 %collective-permute-start.9 = (bf16[5,3,4,8,640]{4,3,2,1,0:T(8,128)(2,1)}, bf16[5,3,4,8,640]{4,3,2,1,0:T(8,128)(2,1)}, u32[]{:S(2)}, u32[]{:S(2)}) collective-permute-start(bf16[5,3,4,8,640]{4,3,2,1,0:T(8,128)(2,1)} %get-tuple-element.48), channel_id=1, source_target_pairs={{0,32},{4,36},{8,40},{12,44},{16,48},{20,52},{24,56},{28,60},{32,6... | collective-permute-start | bytes 1843208 | tf_op jit(solution)/shard_map/ppermute | solution.py:21
  160.0 1.9 collective-permute-start.5
  163.1 1.4 fusion.60
  164.5 18.2 %collective-permute-done.5 = bf16[5,3,4,4,640]{4,3,2,1,0:T(4,128)(2,1)S(1)} collective-permute-done((bf16[5,3,4,4,640]{4,3,2,1,0:T(4,128)(2,1)}, bf16[5,3,4,4,640]{4,3,2,1,0:T(4,128)(2,1)S(1)}, u32[]{:S(2)}, u32[]{:S(2)}) %collective-permute-start.5) | collective-permute-done | bytes 307232 | tf_op jit(solution)/shard_map/ppermute | solution.py:21
  183.4 1.9 collective-permute-start.6
  185.4 3.5 %collective-permute-done.14 = bf16[5,3,4,8,640]{4,3,2,1,0:T(8,128)(2,1)} collective-permute-done((bf16[5,3,4,8,640]{4,3,2,1,0:T(8,128)(2,1)}, bf16[5,3,4,8,640]{4,3,2,1,0:T(8,128)(2,1)}, u32[]{:S(2)}, u32[]{:S(2)}) %collective-permute-start.14) | collective-permute-done | bytes 614432 | tf_op jit(solution)/shard_map/ppermute | solution.py:21
  188.8 1.9 collective-permute-start.4
  190.8 3.9 %collective-permute-start.3 = (bf16[5,3,8,4,640]{4,3,2,1,0:T(4,128)(2,1)}, bf16[5,3,8,4,640]{4,3,2,1,0:T(4,128)(2,1)}, u32[]{:S(2)}, u32[]{:S(2)}) collective-permute-start(bf16[5,3,8,4,640]{4,3,2,1,0:T(4,128)(2,1)} %get-tuple-element.42), channel_id=1, source_target_pairs={{0,4},{4,8},{8,12},{12,16},{16,20},{20,24},{24,28},{28,32},{32,36}... | collective-permute-start | bytes 1843208 | tf_op jit(solution)/shard_map/ppermute | solution.py:21
  194.7 18.3 %collective-permute-start.2 = (bf16[5,3,4,4,640]{4,3,2,1,0:T(4,128)(2,1)}, bf16[5,3,4,4,640]{4,3,2,1,0:T(4,128)(2,1)S(1)}, u32[]{:S(2)}, u32[]{:S(2)}) collective-permute-start(bf16[5,3,4,4,640]{4,3,2,1,0:T(4,128)(2,1)} %get-tuple-element.39), channel_id=1, source_target_pairs={{0,28},{4,32},{8,36},{12,40},{16,44},{20,48},{24,52},{28,56},{32,6... | collective-permute-start | bytes 921608 | tf_op jit(solution)/shard_map/ppermute | solution.py:21
  213.0 2.4 collective-permute-start.1
  215.3 5.7 %maximum_maximum_fusion.1 = bf16[5,3,16,16,640]{4,3,2,1,0:T(8,128)(2,1)S(1)} fusion(bf16[5,3,4,4,640]{4,3,2,1,0:T(4,128)(2,1)} %collective-permute-done.15, bf16[5,3,4,8,640]{4,3,2,1,0:T(8,128)(2,1)} %collective-permute-done.14, bf16[5,3,4,4,640]{4,3,2,1,0:T(4,128)(2,1)} %collective-permute-done.13, bf16[5,3,8,4,640]{4,3,2,1,0:T(4,128)(2,1)} %collective-permute-done.12, ...), kind=kLoop, calls=%fused_computation.1 | loop fusion | flops 49152000 | bytes 9830400 | tf_op jit(solution)/shard_map/concatenate | solution.py:147
  221.8 4.3 %collective-permute-start = (bf16[5,3,4,4,640]{4,3,2,1,0:T(4,128)(2,1)}, bf16[5,3,4,4,640]{4,3,2,1,0:T(4,128)(2,1)}, u32[]{:S(2)}, u32[]{:S(2)}) collective-permute-start(bf16[5,3,4,4,640]{4,3,2,1,0:T(4,128)(2,1)} %get-tuple-element.36), channel_id=1, source_target_pairs={{0,36},{4,40},{8,44},{12,48},{16,52},{20,56},{24,60},{28,64},{32,6... | collective-permute-start | bytes 921608 | tf_op jit(solution)/shard_map/ppermute | solution.py:21
  226.1 2.1 fusion.56
  228.2 2.0 squeeze.51
  230.2 15.5 %collective-permute-done = bf16[5,3,4,4,640]{4,3,2,1,0:T(4,128)(2,1)} collective-permute-done((bf16[5,3,4,4,640]{4,3,2,1,0:T(4,128)(2,1)}, bf16[5,3,4,4,640]{4,3,2,1,0:T(4,128)(2,1)}, u32[]{:S(2)}, u32[]{:S(2)}) %collective-permute-start) | collective-permute-done | bytes 307232 | tf_op jit(solution)/shard_map/ppermute | solution.py:21
  245.7 2.8 collective-permute-done.1
  248.5 5.4 %maximum_maximum_fusion = bf16[5,3,16,16,640]{4,3,2,1,0:T(8,128)(2,1)S(1)} fusion(bf16[5,3,4,4,640]{4,3,2,1,0:T(4,128)(2,1)} %collective-permute-done.7, bf16[5,3,4,8,640]{4,3,2,1,0:T(8,128)(2,1)S(1)} %collective-permute-done.6, bf16[5,3,4,4,640]{4,3,2,1,0:T(4,128)(2,1)S(1)} %copy-done.16, bf16[5,3,8,4,640]{4,3,2,1,0:T(4,128)(2,1)} %collective-permute-done.4, ...), kind=kLoop, calls=%fused_computation | loop fusion | flops 44236800 | bytes 9830400 | tf_op jit(solution)/shard_map/concatenate | solution.py:147
  253.9 2.0 fusion.57
  255.9 2.6 squeeze.44
  258.5 3.5 %squeeze.46 = bf16[768,5,128]{2,1,0:T(8,128)(2,1)} reshape(bf16[1,3,16,16,640]{4,3,2,1,0:T(8,128)(2,1)} %get-tuple-element.32) | data formatting | bytes 1966080 | tf_op jit(solution)/shard_map/squeeze | solution.py:76
  262.1 2.1 fusion.25
  264.2 2.2 fusion.22
  266.4 2.6 squeeze.48
  269.0 2.2 fusion.19
  271.2 2.0 squeeze.41
  273.2 2.0 fusion.28
  275.1 3.5 %squeeze.50 = bf16[768,5,128]{2,1,0:T(8,128)(2,1)} reshape(bf16[1,3,16,16,640]{4,3,2,1,0:T(8,128)(2,1)} %get-tuple-element.30) | data formatting | bytes 1966080 | tf_op jit(solution)/shard_map/squeeze | solution.py:76
  278.7 3.5 %squeeze.49 = bf16[768,5,128]{2,1,0:T(8,128)(2,1)} reshape(bf16[1,3,16,16,640]{4,3,2,1,0:T(8,128)(2,1)} %get-tuple-element.26) | data formatting | bytes 1966080 | tf_op jit(solution)/shard_map/squeeze | solution.py:88
  282.2 3.5 %squeeze.47 = bf16[768,5,128]{2,1,0:T(8,128)(2,1)} reshape(bf16[1,3,16,16,640]{4,3,2,1,0:T(8,128)(2,1)} %get-tuple-element.27) | data formatting | bytes 1966080 | tf_op jit(solution)/shard_map/squeeze | solution.py:88
  285.6 3.5 %squeeze.45 = bf16[768,5,128]{2,1,0:T(8,128)(2,1)} reshape(bf16[1,3,16,16,640]{4,3,2,1,0:T(8,128)(2,1)} %get-tuple-element.28) | data formatting | bytes 1966080 | tf_op jit(solution)/shard_map/squeeze | solution.py:88
  289.1 6.1 %fusion.4 = (f32[5,192]{1,0:T(8,128)S(1)}, f32[5,192]{1,0:T(8,128)S(1)}, f32[5,192]{1,0:T(8,128)S(1)}, f32[5,192]{1,0:T(8,128)S(1)}, f32[5,192]{1,0:T(8,128)S(1)}, /*index=5*/f32[5,192,768]{2,1,0:T(8,128)S(1)}) fusion(pred[768]{0:T(1024)(128)(4,1)S(1)} %reshape.476, f32[5,192,768]{2,1,0:T(8,128)} %fusion.25, f32[5,192,768]{2,1,0:T(8,128)} %fusion.22, ...), kind=kOutput, calls=%fused_computation.28 | convolution fusion | flops 199798080 | bytes 15994368 | tf_op jit(solution)/shard_map/qhd,khd->hqk/dot_general | solution.py:75
  295.3 1.8 convolution_bitcast_fusion.1
  297.8 1.8 convolution_bitcast_fusion.2
  299.6 1.8 convolution_bitcast_fusion
  301.4 3.8 %convert_reduce_fusion.4 = (f32[5,192]{1,0:T(8,128)S(1)}, f32[5,192]{1,0:T(8,128)S(1)}, f32[5,192]{1,0:T(8,128)S(1)}, f32[5,192]{1,0:T(8,128)S(1)}, f32[5,192]{1,0:T(8,128)S(1)}) fusion(f32[5,192]{1,0:T(8,128)S(1)} %get-tuple-element.14, f32[5,192,768]{2,1,0:T(8,128)S(1)} %fusion.28, pred[768]{0:T(1024)(128)(4,1)S(1)} %reshape.476, ...), kind=kLoop, calls=%fused_computation.13 | loop fusion | flops 22113600 | bytes 14784768 | tf_op jit(solution)/shard_map/reduce_sum | solution.py:90
  305.3 1.8 convolution_bitcast_fusion.3
  307.1 3.5 %squeeze.43 = bf16[768,5,128]{2,1,0:T(8,128)(2,1)} reshape(bf16[1,3,16,16,640]{4,3,2,1,0:T(8,128)(2,1)} %get-tuple-element.24) | data formatting | bytes 1966080 | tf_op jit(solution)/shard_map/squeeze | solution.py:88
  310.6 3.5 %fusion.14 = bf16[192,5,128]{2,0,1:T(8,128)(2,1)S(1)} fusion(f32[192,5,128]{2,0,1:T(8,128)} %convolution_bitcast_fusion, f32[192,5,128]{2,0,1:T(8,128)} %convolution_bitcast_fusion.1, f32[192,5,128]{2,0,1:T(8,128)} %convolution_bitcast_fusion.2, f32[192,5,128]{2,0,1:T(8,128)} %convolution_bitcast_fusion.3, bf16[768,5,128]{2,1,0:T(8,128)(2,1)} %squeeze.43, ...), kind=kOutput, calls=%fused_computation.45 | convolution fusion | flops 192921600 | bytes 6167808 | tf_op jit(solution)/shard_map/hqk,khd->hqd/dot_general | solution.py:87
  (105 shorter events, 22.2 us)
Async XLA Ops:
  21.8 9.0 %copy-start.20 = (s32[1,2]{1,0:T(1,128)S(1)}, s32[1,2]{1,0:T(1,128)}, u32[]{:S(2)}) copy-start(s32[1,2]{1,0:T(1,128)} %param.15) | copy-start | bytes 28
  21.8 12.2 %copy-start.18 = (bf16[1,192,640]{2,1,0:T(8,128)(2,1)S(1)}, bf16[1,192,640]{2,1,0:T(8,128)(2,1)}, u32[]{:S(2)}) copy-start(bf16[1,192,640]{2,1,0:T(8,128)(2,1)} %param.8) | copy-start | bytes 737284
  21.8 14.2 %copy-start.19 = (bf16[1,192,640]{2,1,0:T(8,128)(2,1)S(1)}, bf16[1,192,640]{2,1,0:T(8,128)(2,1)}, u32[]{:S(2)}) copy-start(bf16[1,192,640]{2,1,0:T(8,128)(2,1)} %param.9) | copy-start | bytes 737284
  26.0 11.8 %copy-start.13 = (bf16[1,1,192,2560]{3,2,1,0:T(8,128)(2,1)S(1)}, bf16[1,1,192,2560]{3,2,1,0:T(8,128)(2,1)}, u32[]{:S(2)}) copy-start(bf16[1,1,192,2560]{3,2,1,0:T(8,128)(2,1)} %param.11) | copy-start | bytes 2949124
  26.0 48.2 %all-to-all-start.1 = ((bf16[4,2,61440]{2,1,0:T(2,128)(2,1)}), bf16[4,2,61440]{2,1,0:T(2,128)(2,1)}, u32[]{:S(2)}, u32[]{:S(2)}) async-start(bf16[4,2,61440]{2,1,0:T(2,128)(2,1)} %reshape.479), calls=%async_computation.1 | async-start | bytes 1966080 | tf_op jit(solution)/shard_map/all_to_all | solution.py:172
  38.4 1.6 copy-start.21
  44.8 1.3 copy-start.3
  54.3 19.7 %copy-start.22 = (s32[1,9]{1,0:T(1,128)S(1)}, s32[1,9]{1,0:T(1,128)}, u32[]{:S(2)}) copy-start(s32[1,9]{1,0:T(1,128)} %param.14) | copy-start | bytes 112
  69.8 8.1 %copy-start.4 = (f32[192,5,128]{2,0,1:T(8,128)S(1)}, f32[192,5,128]{2,0,1:T(8,128)}, u32[]{:S(2)}) copy-start(f32[192,5,128]{2,0,1:T(8,128)} %convert_element_type.122) | copy-start | bytes 1474564
  74.2 48.4 %all-to-all-start = ((bf16[4,2,61440]{2,1,0:T(2,128)(2,1)}), bf16[4,2,61440]{2,1,0:T(2,128)(2,1)S(1)}, u32[]{:S(2)}, u32[]{:S(2)}) async-start(bf16[4,2,61440]{2,1,0:T(2,128)(2,1)} %reshape.481), calls=%async_computation | async-start | bytes 1966080 | tf_op jit(solution)/shard_map/all_to_all | solution.py:171
  83.3 7.7 %copy-start.6 = (bf16[1,192,640]{2,1,0:T(8,128)(2,1)S(1)}, bf16[1,192,640]{2,1,0:T(8,128)(2,1)}, u32[]{:S(2)}) copy-start(bf16[1,192,640]{2,1,0:T(8,128)(2,1)} %param.10) | copy-start | bytes 737284
  92.4 50.6 %collective-permute-start.15 = (bf16[5,3,4,4,640]{4,3,2,1,0:T(4,128)(2,1)}, bf16[5,3,4,4,640]{4,3,2,1,0:T(4,128)(2,1)}, u32[]{:S(2)}, u32[]{:S(2)}) collective-permute-start(bf16[5,3,4,4,640]{4,3,2,1,0:T(4,128)(2,1)} %get-tuple-element.47), channel_id=1, source_target_pairs={{36,0},{40,4},{44,8},{48,12},{52,16},{56,20},{60,24},{64,28},{68,3... | collective-permute-start | bytes 921608 | tf_op jit(solution)/shard_map/ppermute | solution.py:21
  100.2 44.9 %collective-permute-start.13 = (bf16[5,3,4,4,640]{4,3,2,1,0:T(4,128)(2,1)}, bf16[5,3,4,4,640]{4,3,2,1,0:T(4,128)(2,1)}, u32[]{:S(2)}, u32[]{:S(2)}) collective-permute-start(bf16[5,3,4,4,640]{4,3,2,1,0:T(4,128)(2,1)} %get-tuple-element.46), channel_id=1, source_target_pairs={{28,0},{32,4},{36,8},{40,12},{44,16},{48,20},{52,24},{56,28},{60,3... | collective-permute-start | bytes 921608 | tf_op jit(solution)/shard_map/ppermute | solution.py:21
  102.4 49.8 %collective-permute-start.10 = (bf16[5,3,4,4,640]{4,3,2,1,0:T(4,128)(2,1)}, bf16[5,3,4,4,640]{4,3,2,1,0:T(4,128)(2,1)}, u32[]{:S(2)}, u32[]{:S(2)}) collective-permute-start(bf16[5,3,4,4,640]{4,3,2,1,0:T(4,128)(2,1)} %get-tuple-element.45), channel_id=1, source_target_pairs={{0,28},{4,32},{8,36},{12,40},{16,44},{20,48},{24,52},{28,56},{32,6... | collective-permute-start | bytes 921608 | tf_op jit(solution)/shard_map/ppermute | solution.py:21
  107.7 46.5 %collective-permute-start.8 = (bf16[5,3,4,4,640]{4,3,2,1,0:T(4,128)(2,1)}, bf16[5,3,4,4,640]{4,3,2,1,0:T(4,128)(2,1)}, u32[]{:S(2)}, u32[]{:S(2)}) collective-permute-start(bf16[5,3,4,4,640]{4,3,2,1,0:T(4,128)(2,1)} %get-tuple-element.44), channel_id=1, source_target_pairs={{0,36},{4,40},{8,44},{12,48},{16,52},{20,56},{24,60},{28,64},{32,6... | collective-permute-start | bytes 921608 | tf_op jit(solution)/shard_map/ppermute | solution.py:21
  135.2 24.4 %copy-start.11 = (bf16[192,5,22]{2,0,1:T(8,128)(2,1)S(1)}, bf16[192,5,22]{2,0,1:T(8,128)(2,1)}, u32[]{:S(2)}) copy-start(bf16[192,5,22]{2,0,1:T(8,128)(2,1)} %get-tuple-element.54) | copy-start | bytes 126724
  135.2 24.5 %copy-start.12 = (bf16[192,5,22]{2,0,1:T(8,128)(2,1)S(1)}, bf16[192,5,22]{2,0,1:T(8,128)(2,1)}, u32[]{:S(2)}) copy-start(bf16[192,5,22]{2,0,1:T(8,128)(2,1)} %get-tuple-element.55) | copy-start | bytes 126724
  135.2 24.5 %copy-start.14 = (bf16[192,5,84]{2,0,1:T(8,128)(2,1)S(1)}, bf16[192,5,84]{2,0,1:T(8,128)(2,1)}, u32[]{:S(2)}) copy-start(bf16[192,5,84]{2,0,1:T(8,128)(2,1)} %slice.179) | copy-start | bytes 483844
  135.2 24.8 %collective-permute-start.7 = (bf16[5,3,4,4,640]{4,3,2,1,0:T(4,128)(2,1)}, bf16[5,3,4,4,640]{4,3,2,1,0:T(4,128)(2,1)}, u32[]{:S(2)}, u32[]{:S(2)}) collective-permute-start(bf16[5,3,4,4,640]{4,3,2,1,0:T(4,128)(2,1)} %get-tuple-element.37), channel_id=1, source_target_pairs={{36,0},{40,4},{44,8},{48,12},{52,16},{56,20},{60,24},{64,28},{68,3... | collective-permute-start | bytes 921608 | tf_op jit(solution)/shard_map/ppermute | solution.py:21
  143.0 45.8 %collective-permute-start.14 = (bf16[5,3,4,8,640]{4,3,2,1,0:T(8,128)(2,1)}, bf16[5,3,4,8,640]{4,3,2,1,0:T(8,128)(2,1)}, u32[]{:S(2)}, u32[]{:S(2)}) collective-permute-start(bf16[5,3,4,8,640]{4,3,2,1,0:T(8,128)(2,1)} %get-tuple-element.49), channel_id=1, source_target_pairs={{32,0},{36,4},{40,8},{44,12},{48,16},{52,20},{56,24},{60,28},{64,3... | collective-permute-start | bytes 1843208 | tf_op jit(solution)/shard_map/ppermute | solution.py:21
  145.1 45.7 %collective-permute-start.12 = (bf16[5,3,8,4,640]{4,3,2,1,0:T(4,128)(2,1)}, bf16[5,3,8,4,640]{4,3,2,1,0:T(4,128)(2,1)}, u32[]{:S(2)}, u32[]{:S(2)}) collective-permute-start(bf16[5,3,8,4,640]{4,3,2,1,0:T(4,128)(2,1)} %get-tuple-element.51), channel_id=1, source_target_pairs={{4,0},{8,4},{12,8},{16,12},{20,16},{24,20},{28,24},{32,28},{36,32}... | collective-permute-start | bytes 1843208 | tf_op jit(solution)/shard_map/ppermute | solution.py:21
  152.3 42.4 %collective-permute-start.11 = (bf16[5,3,8,4,640]{4,3,2,1,0:T(4,128)(2,1)}, bf16[5,3,8,4,640]{4,3,2,1,0:T(4,128)(2,1)}, u32[]{:S(2)}, u32[]{:S(2)}) collective-permute-start(bf16[5,3,8,4,640]{4,3,2,1,0:T(4,128)(2,1)} %get-tuple-element.50), channel_id=1, source_target_pairs={{0,4},{4,8},{8,12},{12,16},{16,20},{20,24},{24,28},{28,32},{32,36}... | collective-permute-start | bytes 1843208 | tf_op jit(solution)/shard_map/ppermute | solution.py:21
  154.2 58.8 %collective-permute-start.9 = (bf16[5,3,4,8,640]{4,3,2,1,0:T(8,128)(2,1)}, bf16[5,3,4,8,640]{4,3,2,1,0:T(8,128)(2,1)}, u32[]{:S(2)}, u32[]{:S(2)}) collective-permute-start(bf16[5,3,4,8,640]{4,3,2,1,0:T(8,128)(2,1)} %get-tuple-element.48), channel_id=1, source_target_pairs={{0,32},{4,36},{8,40},{12,44},{16,48},{20,52},{24,56},{28,60},{32,6... | collective-permute-start | bytes 1843208 | tf_op jit(solution)/shard_map/ppermute | solution.py:21
  160.0 22.7 %collective-permute-start.5 = (bf16[5,3,4,4,640]{4,3,2,1,0:T(4,128)(2,1)}, bf16[5,3,4,4,640]{4,3,2,1,0:T(4,128)(2,1)S(1)}, u32[]{:S(2)}, u32[]{:S(2)}) collective-permute-start(bf16[5,3,4,4,640]{4,3,2,1,0:T(4,128)(2,1)} %get-tuple-element.38), channel_id=1, source_target_pairs={{28,0},{32,4},{36,8},{40,12},{44,16},{48,20},{52,24},{56,28},{60,3... | collective-permute-start | bytes 921608 | tf_op jit(solution)/shard_map/ppermute | solution.py:21
  182.7 0.7 copy-start.15
  183.4 62.3 %collective-permute-start.6 = (bf16[5,3,4,8,640]{4,3,2,1,0:T(8,128)(2,1)}, bf16[5,3,4,8,640]{4,3,2,1,0:T(8,128)(2,1)S(1)}, u32[]{:S(2)}, u32[]{:S(2)}) collective-permute-start(bf16[5,3,4,8,640]{4,3,2,1,0:T(8,128)(2,1)} %get-tuple-element.41), channel_id=1, source_target_pairs={{32,0},{36,4},{40,8},{44,12},{48,16},{52,20},{56,24},{60,28},{64,3... | collective-permute-start | bytes 1843208 | tf_op jit(solution)/shard_map/ppermute | solution.py:21
  188.8 56.9 %collective-permute-start.4 = (bf16[5,3,8,4,640]{4,3,2,1,0:T(4,128)(2,1)}, bf16[5,3,8,4,640]{4,3,2,1,0:T(4,128)(2,1)}, u32[]{:S(2)}, u32[]{:S(2)}) collective-permute-start(bf16[5,3,8,4,640]{4,3,2,1,0:T(4,128)(2,1)} %get-tuple-element.43), channel_id=1, source_target_pairs={{4,0},{8,4},{12,8},{16,12},{20,16},{24,20},{28,24},{32,28},{36,32}... | collective-permute-start | bytes 1843208 | tf_op jit(solution)/shard_map/ppermute | solution.py:21
  190.8 54.9 %collective-permute-start.3 = (bf16[5,3,8,4,640]{4,3,2,1,0:T(4,128)(2,1)}, bf16[5,3,8,4,640]{4,3,2,1,0:T(4,128)(2,1)}, u32[]{:S(2)}, u32[]{:S(2)}) collective-permute-start(bf16[5,3,8,4,640]{4,3,2,1,0:T(4,128)(2,1)} %get-tuple-element.42), channel_id=1, source_target_pairs={{0,4},{4,8},{8,12},{12,16},{16,20},{20,24},{24,28},{28,32},{32,36}... | collective-permute-start | bytes 1843208 | tf_op jit(solution)/shard_map/ppermute | solution.py:21
  194.7 26.4 %collective-permute-start.2 = (bf16[5,3,4,4,640]{4,3,2,1,0:T(4,128)(2,1)}, bf16[5,3,4,4,640]{4,3,2,1,0:T(4,128)(2,1)S(1)}, u32[]{:S(2)}, u32[]{:S(2)}) collective-permute-start(bf16[5,3,4,4,640]{4,3,2,1,0:T(4,128)(2,1)} %get-tuple-element.39), channel_id=1, source_target_pairs={{0,28},{4,32},{8,36},{12,40},{16,44},{20,48},{24,52},{28,56},{32,6... | collective-permute-start | bytes 921608 | tf_op jit(solution)/shard_map/ppermute | solution.py:21
  213.0 35.5 %collective-permute-start.1 = (bf16[5,3,4,8,640]{4,3,2,1,0:T(8,128)(2,1)}, bf16[5,3,4,8,640]{4,3,2,1,0:T(8,128)(2,1)}, u32[]{:S(2)}, u32[]{:S(2)}) collective-permute-start(bf16[5,3,4,8,640]{4,3,2,1,0:T(8,128)(2,1)} %get-tuple-element.40), channel_id=1, source_target_pairs={{0,32},{4,36},{8,40},{12,44},{16,48},{20,52},{24,56},{28,60},{32,6... | collective-permute-start | bytes 1843208 | tf_op jit(solution)/shard_map/ppermute | solution.py:21
  221.1 0.7 copy-start.17
  221.8 26.7 %copy-start.16 = (bf16[5,3,4,4,640]{4,3,2,1,0:T(4,128)(2,1)S(1)}, bf16[5,3,4,4,640]{4,3,2,1,0:T(4,128)(2,1)}, u32[]{:S(2)}) copy-start(bf16[5,3,4,4,640]{4,3,2,1,0:T(4,128)(2,1)} %copy-done.15) | copy-start | bytes 921604
  221.8 23.9 %collective-permute-start = (bf16[5,3,4,4,640]{4,3,2,1,0:T(4,128)(2,1)}, bf16[5,3,4,4,640]{4,3,2,1,0:T(4,128)(2,1)}, u32[]{:S(2)}, u32[]{:S(2)}) collective-permute-start(bf16[5,3,4,4,640]{4,3,2,1,0:T(4,128)(2,1)} %get-tuple-element.36), channel_id=1, source_target_pairs={{0,36},{4,40},{8,44},{12,48},{16,52},{20,56},{24,60},{28,64},{32,6... | collective-permute-start | bytes 921608 | tf_op jit(solution)/shard_map/ppermute | solution.py:21
  262.1 2.1 copy-start.5
  289.1 6.2 %copy-start.2 = (f32[5,192,768]{2,1,0:T(8,128)S(1)}, f32[5,192,768]{2,1,0:T(8,128)}, u32[]{:S(2)}) copy-start(f32[5,192,768]{2,1,0:T(8,128)} %fusion.19) | copy-start | bytes 8847364
  289.1 6.2 %copy-start.9 = (bf16[768,5,128]{2,1,0:T(8,128)(2,1)S(1)}, bf16[768,5,128]{2,1,0:T(8,128)(2,1)}, u32[]{:S(2)}) copy-start(bf16[768,5,128]{2,1,0:T(8,128)(2,1)} %squeeze.49) | copy-start | bytes 2949124
  295.3 1.8 copy-start.1
  295.3 2.5 copy-start.10
  297.8 1.8 copy-start.7
  299.6 1.8 copy-start
  301.4 3.8 %copy-start.8 = (bf16[768,5,128]{2,1,0:T(8,128)(2,1)S(1)}, bf16[768,5,128]{2,1,0:T(8,128)(2,1)}, u32[]{:S(2)}) copy-start(bf16[768,5,128]{2,1,0:T(8,128)(2,1)} %squeeze.45) | copy-start | bytes 2949124
where the time goes:
time: 321 us; the launch traced here: 315 us
  starting transfers between devices  94.4 us (29%)
  local copies, waits for them, and re-layouts  93 us (29%)
  other arithmetic  58.6 us (18%)
  waiting for transfers between devices  40 us (12%)
  matrix products  25.4 us (8%)
  between operations  4.07 us (1%)
    ppermute x16, starting transfers between devices, passed_along(): return lax.ppermute(x, axis, pairs)  86.1 us
    ppermute x16, waiting for transfers between devices, passed_along(): return lax.ppermute(x, axis, pairs)  40 us
    unnamed x2, other arithmetic  31 us
    unnamed x54, local copies, waits for them, and re-layouts  19.4 us
    squeeze x5, local copies, waits for them, and re-layouts, attend_blocks(): block_values[number]  16 us
    dot_general x5, matrix products, attend_blocks(): jnp.einsum('qhd,khd->hqk', rotated, block_keys[number], preferred_element...  14.6 us
    squeeze x5, local copies, waits for them, and re-layouts, attend_blocks(): block_keys[number]  14.2 us
    dot_general x5, matrix products, attend_blocks(): jnp.einsum('hqk,khd->hqd', weights, block_values[number], preferred_eleme...  10.8 us
  transfers between devices with their start and end apart: 18, of which 4 were waited for; matrix products, arithmetic and copies ran while one was open for 25% of the time, Pallas kernels for 0%

commit v1 on v0

v1 whole, which is shorter than its diff:
```python
import functools
import math

import jax
import jax.numpy as jnp
from jax import lax
from jax.experimental import pallas as pl
from jax.experimental.pallas import tpu as pltpu
from jax.sharding import PartitionSpec as P

TH = 8
TW = 8
F = 3
HALO = 4
GX = 8
HD = 128
PAIRS = 22
TOKT = 192
STRETCHES = 4
HALF = 48
ROUNDS = 5
GROUPS = 4
BLOCKS = GROUPS + 1
NEGATIVE = -1e30
SCALE = math.log2(math.e) / math.sqrt(HD)
MESH = pl.DeviceIdType.MESH
O, U, D = 0, 1, 2
(
    Z_RIGHT,
    Z_LEFT,
    Q_CHIP,
    Q_UP,
    Q_DOWN,
    Q_PASS,
    Q_CORE0,
    Q_CORE2,
    P_CORE,
    L_CORE,
    P_CHIP,
    L_CHIP,
    P_UP,
    L_UP,
    P_DOWN,
    L_DOWN,
    MESSAGES,
) = range(17)


def nt_dot(a, b):
    return lax.dot_general(a, b, (((1,), (1,)), ((), ())), preferred_element_type=jnp.float32)


def dot(a, b):
    return lax.dot_general(a, b, (((1,), (0,)), ((), ())), preferred_element_type=jnp.float32)


def iota(shape, dim):
    return lax.broadcasted_iota(jnp.int32, shape, dim)


def spread(rows):
    padded = jnp.concatenate([rows, jnp.zeros((HD - rows.shape[0], 256), jnp.float32)], axis=0)
    return padded.T[:TOKT]


def gathered(columns):
    padded = jnp.concatenate([columns, jnp.zeros((256 - TOKT, HD), jnp.float32)], axis=0)
    return padded.T[:8]


def kernel(
    grid_rows,
    order_ref,
    mask_ref,
    reach_ref,
    q_hbm,
    k_hbm,
    v_hbm,
    ck_hbm,
    cv_hbm,
    out_ref,
    q_in,
    k_in,
    v_in,
    ck_in,
    cv_in,
    kv,
    q,
    par,
    par_up,
    par_down,
    bias,
    table,
    part,
    lse,
    p1_send,
    p1_recv,
    l1_send,
    l1_recv,
    p2_keep,
    p2_send,
    p2_recv,
    l2_keep,
    l2_send,
    l2_recv,
    p3_keep,
    p3_send,
    p3_recv,
    l3_keep,
    l3_recv,
    in_sem,
    par_send_sem,
    par_recv_sem,
    send_sem,
    recv_sem,
):
    tile = lax.axis_index("tile")
    slot = lax.axis_index("slot")
    row, col = tile // GX, lax.rem(tile, GX)
    tiles = grid_rows * GX
    core_slot = slot + 1 - 2 * lax.rem(slot, 2)
    chip_slot = lax.rem(slot + 2, 4)
    right = row * GX + lax.rem(col + 1, GX)
    left = row * GX + lax.rem(col + GX - 1, GX)
    up = lax.rem(tile + tiles - GX, tiles)
    down = lax.rem(tile + GX, tiles)
    core_mate, chip_mate = (tile, core_slot), (tile, chip_slot)
    at_right, at_left = (right, slot), (left, slot)
    at_up, at_down = (up, chip_slot), (down, chip_slot)

    inputs = [
        pltpu.make_async_copy(source, target, in_sem.at[n])
        for n, (source, target) in enumerate(
            ((ck_hbm, ck_in), (cv_hbm, cv_in), (k_hbm, k_in), (v_hbm, v_in), (q_hbm, q_in))
        )
    ]
    for copy in inputs:
        copy.start()

    barrier = pltpu.get_barrier_semaphore()
    partners = (core_mate, chip_mate, at_right, at_left, at_up, at_down)
    for partner in partners:
        pl.semaphore_signal(barrier, inc=1, device_id=partner, device_id_type=MESH)

    def message(number, h, source, target, device):
        return pltpu.make_async_remote_copy(
            src_ref=source,
            dst_ref=target,
            send_sem=send_sem.at[number, h],
            recv_sem=recv_sem.at[number, h],
            device_id=device,
            device_id_type=MESH,
        )

    messages = {
        Z_RIGHT: lambda h: message(Z_RIGHT, h, kv.at[h, 2], kv.at[h, 0], at_right),
        Z_LEFT: lambda h: message(Z_LEFT, h, kv.at[h, 1], kv.at[h, 3], at_left),
        Q_CHIP: lambda h: message(Q_CHIP, h, q.at[h, 0, O], q.at[h, 2, O], chip_mate),
        Q_UP: lambda h: message(Q_UP, h, q.at[h, 0, O], q.at[h, 2, D], at_up),
        Q_DOWN: lambda h: message(Q_DOWN, h, q.at[h, 0, O], q.at[h, 2, U], at_down),
        Q_PASS: lambda h: message(
            Q_PASS, h, q.at[h, 2, pl.ds(U, 2)], q.at[h, 0, pl.ds(U, 2)], chip_mate
        ),
        Q_CORE0: lambda h: message(Q_CORE0, h, q.at[h, 0], q.at[h, 1], core_mate),
        Q_CORE2: lambda h: message(Q_CORE2, h, q.at[h, 2], q.at[h, 3], core_mate),
        P_CORE: lambda h: message(P_CORE, h, p1_send.at[h], p1_recv.at[h], core_mate),
        L_CORE: lambda h: message(L_CORE, h, l1_send.at[h], l1_recv.at[h], core_mate),
        P_CHIP: lambda h: message(P_CHIP, h, p2_send.at[h], p2_recv.at[h], chip_mate),
        L_CHIP: lambda h: message(L_CHIP, h, l2_send.at[h], l2_recv.at[h], chip_mate),
        P_UP: lambda h: message(P_UP, h, p3_send.at[h, 0], p3_recv.at[h, 0], at_up),
        L_UP: lambda h: message(L_UP, h, l3_keep.at[h], l3_recv.at[h, 0], at_up),
        P_DOWN: lambda h: message(P_DOWN, h, p3_send.at[h, 1], p3_recv.at[h, 1], at_down),
        L_DOWN: lambda h: message(L_DOWN, h, l3_keep.at[h], l3_recv.at[h, 1], at_down),
    }

    def start(h, *numbers):
        for number in numbers:
            messages[number](h).start()

    def arrived(h, *numbers):
        for number in numbers:
            messages[number](h).wait_recv()

    age = jnp.int32(0)
    for n in range(STRETCHES):
        age = age + jnp.where(slot == n, order_ref[n], 0)
    sub, lane = iota((8, HD), 0), iota((8, HD), 1)
    moment = jnp.where(sub < F, (STRETCHES - 1 - age) * F + sub, STRETCHES * F + sub - F)
    pair = jnp.where(lane < PAIRS, lane, lane - PAIRS).astype(jnp.float32)
    frequency = jnp.exp(pair * (-math.log(10000.0) / PAIRS))
    angle = jnp.where(lane < 2 * PAIRS, moment.astype(jnp.float32) * frequency, 0.0)
    cosine, sine = jnp.cos(angle), jnp.sin(angle)
    for n in range(2):
        for f in range(F):
            for at, values in ((0, cosine), (1, sine)):
                wanted = jnp.broadcast_to(values[n * F + f : n * F + f + 1], (16, HD))
                for quarter in range(4):
                    table[n, at, pl.ds(quarter * HALF + f * 16, 16)] = wanted
                if n == 1:
                    for part_at in range(4):
                        table[2, at, pl.ds(f * 64 + part_at * 16, 16)] = wanted

    first, second = iota((HD, HD), 0), iota((HD, HD), 1)
    exchange = jnp.where(
        (second < PAIRS) & (first == second + PAIRS),
        -1.0,
        jnp.where((second >= PAIRS) & (second < 2 * PAIRS) & (first == second - PAIRS), 1.0, 0.0),
    ).astype(jnp.bfloat16)
    at = iota((TOKT, TOKT), 0)
    side = (at >= 2 * HALF).astype(jnp.int32)
    rest = at - side * 2 * HALF
    lower = (rest >= HALF).astype(jnp.int32)
    rest = rest - lower * HALF
    source = (
        (rest >> 4) * TH * TW + (lower * HALO + ((rest >> 2) & 3)) * TW + side * HALO + (rest & 3)
    )
    quarters = (iota((TOKT, TOKT), 1) == source).astype(jnp.float32).astype(jnp.bfloat16)

    def turned(x, n):
        swapped = dot(x.astype(jnp.bfloat16), exchange)
        return x.astype(jnp.float32) * table[n, 0] + swapped * table[n, 1]

    def group_of(e):
        if e == 0:
            return slot
        if e == 1:
            return core_slot
        if e == 2:
            return chip_slot
        return 3 - slot

    def prepare_block(h, e, keys, values, n):
        both = dot(quarters, jnp.concatenate([keys, values], axis=1))
        new_keys = turned(both[:, :HD], n).astype(jnp.bfloat16)
        new_values = both[:, HD:].astype(jnp.bfloat16)
        for g in range(2):
            for lower_half in range(2):
                at_row = (g * 2 + lower_half) * HALF
                kv[h, 1 + g, 0, e, lower_half] = new_keys[at_row : at_row + HALF]
                kv[h, 1 + g, 1, e, lower_half] = new_values[at_row : at_row + HALF]

    def prepare(h):
        for e in range(GROUPS):
            lanes = pl.ds(pl.multiple_of((group_of(e) * ROUNDS + h) * HD, HD), HD)
            prepare_block(h, e, ck_in[0, 0, :, lanes], cv_in[0, 0, :, lanes], 0)
        lanes = pl.ds(pl.multiple_of(h * HD, HD), HD)
        prepare_block(h, GROUPS, k_in[0, :, lanes], v_in[0, :, lanes], 1)
        q[h, 0, O] = turned(q_in[0, :, lanes], 2).astype(jnp.bfloat16)

    entry = iota((16, HD), 0)
    block = jnp.zeros((16, HD), jnp.int32)
    for n in range(9):
        block = jnp.where(entry == n, mask_ref[0, n], block)
    for n in range(2):
        block = jnp.where(entry == 9 + n, reach_ref[0, n], block)
    par[...] = block

    for copy in inputs:
        copy.wait()
    pl.semaphore_wait(barrier, len(partners))

    par_copies = [
        pltpu.make_async_remote_copy(
            src_ref=par,
            dst_ref=target,
            send_sem=par_send_sem.at[n],
            recv_sem=par_recv_sem.at[n],
            device_id=device,
            device_id_type=MESH,
        )
        for n, (target, device) in enumerate(((par_up, at_down), (par_down, at_up)))
    ]
    for copy in par_copies:
        copy.start()

    def first_sends(h, carry):
        prepare(h)
        start(h, Z_RIGHT, Z_LEFT, Q_UP, Q_DOWN, Q_CHIP)
        return carry

    lax.fori_loop(0, ROUNDS, first_sends, 0)

    for copy in par_copies:
        copy.wait_recv()

    key, feature = iota((TOKT, HD), 0), iota((TOKT, HD), 1)
    from_left, from_right = key < HALF, key >= 3 * HALF
    key_row, key_col = (key >> 2) & 3, key & 3

    def window(values, dy, rows_good):
        bits = [values[(dy + 1) * 3 + n : (dy + 1) * 3 + n + 1] for n in range(3)]
        reach_cols = values[10:11]
        middle = jnp.full((1, HD), 1, jnp.int32) if dy == 0 else bits[1]
        on_left = from_left & (key_col >= HALO - reach_cols) & (bits[0] > 0) & (col >= 1)
        on_right = from_right & (key_col < reach_cols) & (bits[2] > 0) & (col < GX - 1)
        inside = (key >= HALF) & (key < 3 * HALF) & (middle > 0)
        good = (on_left | on_right | inside) & rows_good
        return jnp.where(good, 0.0, NEGATIVE)

    above, below, here = par_up[...], par_down[...], par[...]
    own_window = window(here, 0, key >= 0)
    up_window = window(above, 1, (key_row < above[9:10]) & (row >= 1))
    down_window = window(below, -1, (key_row >= HALO - below[9:10]) & (row < grid_rows - 1))
    for n, other in enumerate((up_window, down_window)):
        bias[n] = jnp.where(
            feature == 0, other, jnp.where(feature == 1, own_window, 0.0)
        ).astype(jnp.bfloat16)

    def pass_on(h):
        arrived(h, Q_UP, Q_DOWN)
        start(h, Q_PASS)

    def share(h):
        arrived(h, Q_CHIP)
        start(h, Q_CORE2)
        arrived(h, Q_PASS)
        start(h, Q_CORE0)

    def attend(queries, marker, keys, values):
        scores = nt_dot(jnp.concatenate([queries, marker], axis=1), keys)
        highest = jnp.max(scores, axis=1, keepdims=True)
        weights = jnp.exp2((scores - highest) * SCALE).astype(jnp.bfloat16)
        summed = dot(weights, values)
        total = summed[:, HD:]
        return summed[:, :HD] / total, highest * SCALE + jnp.log2(total)

    def compute(h):
        other_marker = jnp.where(feature == 0, 1.0, 0.0).astype(jnp.bfloat16)
        own_marker = jnp.where(feature == 1, 1.0, 0.0).astype(jnp.bfloat16)
        ones = jnp.ones((TOKT, HD), jnp.bfloat16)
        kept = jnp.zeros((TOKT, HD), jnp.float32)
        sent = jnp.zeros((TOKT, HD), jnp.float32)
        for e in range(GROUPS):
            keys, values = [[], []], [[], []]
            for block_at in (e,) if e > 0 else (0, GROUPS):
                for lower_half in range(2):
                    these_keys = kv[h, :, 0, block_at, lower_half].reshape(TOKT, HD)
                    these_values = kv[h, :, 1, block_at, lower_half].reshape(TOKT, HD)
                    keys[lower_half].append(
                        jnp.concatenate([these_keys, bias[lower_half]], axis=1)
                    )
                    values[lower_half].append(jnp.concatenate([these_values, ones], axis=1))
            for tile_kind, halves, marker in (
                (U, (0,), other_marker),
                (D, (1,), other_marker),
                (O, (0, 1), own_marker),
            ):
                all_keys = jnp.concatenate([x for n in halves for x in keys[n]], axis=0)
                all_values = jnp.concatenate([x for n in halves for x in values[n]], axis=0)
                result, level = attend(q[h, e, tile_kind], marker, all_keys, all_values)
                place = e // 2 * 3 + tile_kind
                if e % 2 == 0:
                    part[e // 2, tile_kind] = result
                    kept = jnp.where(feature == place, level, kept)
                else:
                    p1_send[h, e // 2, tile_kind] = result.astype(jnp.bfloat16)
                    sent = jnp.where(feature == place, level, sent)
        lse[...] = kept
        l1_send[h] = sent
        start(h, P_CORE, L_CORE)

    def after_core(h):
        arrived(h, P_CORE, L_CORE)
        mine, theirs = lse[...], l1_recv[h]
        newest = jnp.maximum(mine, theirs)
        mine_part, theirs_part = jnp.exp2(mine - newest), jnp.exp2(theirs - newest)
        total = mine_part + theirs_part
        mine_part, theirs_part = mine_part / total, theirs_part / total
        rows = gathered(newest + jnp.log2(total))
        for tile_kind in range(3):
            for n in range(2):
                place = n * 3 + tile_kind
                result = (
                    part[n, tile_kind] * mine_part[:, place : place + 1]
                    + p1_recv[h, n, tile_kind].astype(jnp.float32)
                    * theirs_part[:, place : place + 1]
                )
                if (n == 0) == (tile_kind == O):
                    p2_keep[h, tile_kind] = result
                else:
                    p2_send[h, tile_kind] = result.astype(jnp.bfloat16)
        start(h, P_CHIP)
        l2_keep[h] = rows
        l2_send[h] = jnp.concatenate(
            [rows[3:4], rows[0:1], rows[0:1], rows[0:1], rows[1:2], rows[2:3], rows[0:2]], axis=0
        )
        start(h, L_CHIP)

    def after_chip(h):
        arrived(h, P_CHIP, L_CHIP)
        mine, theirs = l2_keep[h], l2_recv[h]
        newest = jnp.maximum(mine, theirs)
        mine_part, theirs_part = jnp.exp2(mine - newest), jnp.exp2(theirs - newest)
        total = mine_part + theirs_part
        l3_keep[h] = newest + jnp.log2(total)
        start(h, L_UP, L_DOWN)
        columns = spread(jnp.concatenate([mine_part / total, theirs_part / total], axis=0))
        for tile_kind, place in ((U, 4), (D, 5), (O, 0)):
            result = (
                p2_keep[h, tile_kind] * columns[:, place : place + 1]
                + p2_recv[h, tile_kind].astype(jnp.float32) * columns[:, 8 + place : 9 + place]
            )
            if tile_kind == O:
                p3_keep[h] = result
            else:
                p3_send[h, tile_kind - 1] = result.astype(jnp.bfloat16)
                start(h, P_UP if tile_kind == U else P_DOWN)

    def after_row(h):
        arrived(h, P_UP, L_UP, P_DOWN, L_DOWN)
        own = l3_keep[h][0:1]
        from_down = l3_recv[h, 0][4:5]
        from_up = l3_recv[h, 1][5:6]
        newest = jnp.maximum(jnp.maximum(own, from_down), from_up)
        parts = [jnp.exp2(x - newest) for x in (own, from_down, from_up)]
        total = parts[0] + parts[1] + parts[2]
        columns = spread(
            jnp.concatenate(
                [x / total for x in parts] + [jnp.zeros((5, 256), jnp.float32)], axis=0
            )
        )
        result = (
            p3_keep[h] * columns[:, 0:1]
            + p3_recv[h, 0].astype(jnp.float32) * columns[:, 1:2]
            + p3_recv[h, 1].astype(jnp.float32) * columns[:, 2:3]
        )
        lanes = pl.ds(pl.multiple_of(h * HD, HD), HD)
        out_ref[0, :, lanes] = result.astype(jnp.bfloat16)

    pass_on(0)
    share(0)

    def step(i, carry):
        @pl.when(i + 1 < ROUNDS)
        def _():
            pass_on(i + 1)

        @pl.when((i >= 1) & (i <= ROUNDS))
        def _():
            after_core(i - 1)

        @pl.when((i >= 2) & (i <= ROUNDS + 1))
        def _():
            after_chip(i - 2)

        @pl.when(i >= 3)
        def _():
            after_row(i - 3)

        @pl.when(i + 1 < ROUNDS)
        def _():
            share(i + 1)

        @pl.when(i < ROUNDS)
        def _():
            arrived(i, Q_CORE0, Q_CORE2, Z_RIGHT, Z_LEFT)
            compute(i)

        return carry

    lax.fori_loop(0, ROUNDS + 3, step, 0)

    def finish(h, carry):
        for number in range(MESSAGES):
            messages[number](h).wait_send()
        return carry

    lax.fori_loop(0, ROUNDS, finish, 0)
    for copy in par_copies:
        copy.wait_send()


def solution(mesh):
    grid_rows = mesh.shape["tile"] // GX
    bf16, f32, i32 = jnp.bfloat16, jnp.float32, jnp.int32
    wide = GROUPS * ROUNDS * HD

    def on_device(queries, keys, values, cache_keys, cache_values, order, tile_mask, reach):
        smem = pl.BlockSpec(memory_space=pltpu.SMEM)
        anywhere = pl.BlockSpec(memory_space=pl.ANY)
        piece = (TOKT, HD)
        return pl.pallas_call(
            functools.partial(kernel, grid_rows),
            out_shape=jax.ShapeDtypeStruct((1, TOKT, ROUNDS * HD), bf16),
            in_specs=[smem] * 3 + [anywhere] * 5,
            out_specs=pl.BlockSpec(memory_space=pltpu.VMEM),
            scratch_shapes=[
                pltpu.VMEM((1, TOKT, ROUNDS * HD), bf16),
                pltpu.VMEM((1, TOKT, ROUNDS * HD), bf16),
                pltpu.VMEM((1, TOKT, ROUNDS * HD), bf16),
                pltpu.VMEM((1, 1, TOKT, wide), bf16),
                pltpu.VMEM((1, 1, TOKT, wide), bf16),
                pltpu.VMEM((ROUNDS, 4, 2, BLOCKS, 2, HALF, HD), bf16),
                pltpu.VMEM((ROUNDS, GROUPS, 3) + piece, bf16),
                pltpu.VMEM((16, HD), i32),
                pltpu.VMEM((16, HD), i32),
                pltpu.VMEM((16, HD), i32),
                pltpu.VMEM((2,) + piece, bf16),
                pltpu.VMEM((3, 2) + piece, f32),
                pltpu.VMEM((2, 3) + piece, f32),
                pltpu.VMEM(piece, f32),
                pltpu.VMEM((ROUNDS, 2, 3) + piece, bf16),
                pltpu.VMEM((ROUNDS, 2, 3) + piece, bf16),
                pltpu.VMEM((ROUNDS,) + piece, f32),
                pltpu.VMEM((ROUNDS,) + piece, f32),
                pltpu.VMEM((ROUNDS, 3) + piece, f32),
                pltpu.VMEM((ROUNDS, 3) + piece, bf16),
                pltpu.VMEM((ROUNDS, 3) + piece, bf16),
                pltpu.VMEM((ROUNDS, 8, 256), f32),
                pltpu.VMEM((ROUNDS, 8, 256), f32),
                pltpu.VMEM((ROUNDS, 8, 256), f32),
                pltpu.VMEM((ROUNDS,) + piece, f32),
                pltpu.VMEM((ROUNDS, 2) + piece, bf16),
                pltpu.VMEM((ROUNDS, 2) + piece, bf16),
                pltpu.VMEM((ROUNDS, 8, 256), f32),
                pltpu.VMEM((ROUNDS, 2, 8, 256), f32),
                pltpu.SemaphoreType.DMA((5,)),
                pltpu.SemaphoreType.DMA((2,)),
                pltpu.SemaphoreType.DMA((2,)),
                pltpu.SemaphoreType.DMA((MESSAGES, ROUNDS)),
                pltpu.SemaphoreType.DMA((MESSAGES, ROUNDS)),
            ],
            compiler_params=pltpu.CompilerParams(
                collective_id=0, has_side_effects=True, vmem_limit_bytes=56 * 2**20
            ),
        )(order, tile_mask, reach, queries, keys, values, cache_keys, cache_values)

    placed = (
        P("tile", None, "slot"),
        P("tile", None, "slot"),
        P("tile", None, "slot"),
        P("slot", "tile", None, None),
        P("slot", "tile", None, None),
        P(),
        P("tile", None),
        P("tile", None),
    )
    return jax.shard_map(
        on_device, mesh=mesh, in_specs=placed, out_specs=P("tile", None, "slot"), check_vma=False
    )
```

time: 321 us -> 66.2 us (0.21)
  the two profiles are of different devices: /device:TPU:2 before, /device:TPU:1 now
where the time goes in v1:
time: 66.2 us; the launch traced here: 65.1 us
  Pallas kernels  63.4 us (96%)
  local copies, waits for them, and re-layouts  1.66 us (3%)
    pallas_call x1, Pallas kernels, on_device(): pl.pallas_call(functools.partial(kernel, grid_rows), out_shape=jax.ShapeD...  63.4 us
    unnamed x1, local copies, waits for them, and re-layouts  1.66 us

profile of v1, /device:TPU:1, one launch (start us, length us, event | category | flops | bytes accessed | tf_op | source)
XLA Modules:
  0.0 65.1 jit_solution(8246299383447988740)
XLA Ops:
  0.0 63.4 %shard_map.82 = bf16[1,192,640]{2,1,0:T(8,128)(2,1)} custom-call(s32[4]{0:T(128)} %order_ref.1, s32[1,9]{1,0:T(1,128)} %mask_ref.1, s32[1,2]{1,0:T(1,128)} %reach_ref.1, bf16[1,192,640]{2,1,0:T(8,128)(2,1)} %q_hbm.1, bf16[1,192,640]{2,1,0:T(8,128)(2,1)} %k_hbm.1, bf16[1,192,640]{2,1,0:T(8,128)(2,1)} %v_hbm.1, bf16[1,1,192,2560]{3,2,1,0:T(8,128)(2,1)} %ck_hbm.1, ...), custom_call_target="tpu_custom_call" | custom-call | tf_op jit(solution)/shard_map/pallas_call | solution.py:482
  63.5 1.7 %copy.10 = bf16[1,192,640]{2,1,0:T(8,128)(2,1)} copy(bf16[1,192,640]{2,1,0:T(8,128)(2,1)} %shard_map.82) | data formatting | bytes 491520

commit v2 on v1

--- a/solution.py
+++ b/solution.py
@@ -20,30 +20,36 @@
 HALF = 48
 ROUNDS = 5
 GROUPS = 4
-BLOCKS = GROUPS + 1
 NEGATIVE = -1e30
 SCALE = math.log2(math.e) / math.sqrt(HD)
 MESH = pl.DeviceIdType.MESH
-O, U, D = 0, 1, 2
+U, O, D = 0, 1, 2
 (
-    Z_RIGHT,
-    Z_LEFT,
+    Z_RIGHT0,
+    Z_LEFT0,
+    Z_RIGHT1,
+    Z_LEFT1,
     Q_CHIP,
     Q_UP,
+    Q_UP2,
     Q_DOWN,
     Q_PASS,
     Q_CORE0,
     Q_CORE2,
-    P_CORE,
-    L_CORE,
-    P_CHIP,
-    L_CHIP,
+    P_CORE0,
+    L_CORE0,
+    P_CORE1,
+    L_CORE1,
+    P_CHIP0,
+    L_CHIP0,
+    P_CHIP1,
+    L_CHIP1,
     P_UP,
     L_UP,
     P_DOWN,
     L_DOWN,
     MESSAGES,
-) = range(17)
+) = range(24)
 
 
 def nt_dot(a, b):
@@ -84,7 +90,8 @@
     v_in,
     ck_in,
     cv_in,
-    kv,
+    kv0,
+    kv1,
     q,
     par,
     par_up,
@@ -97,16 +104,17 @@
     p1_recv,
     l1_send,
     l1_recv,
-    p2_keep,
-    p2_send,
-    p2_recv,
-    l2_keep,
-    l2_send,
+    p2_send0,
+    p2_recv0,
+    p2_send1,
+    p2_recv1,
+    keep0,
+    keep1,
+    l2_rows,
     l2_recv,
-    p3_keep,
     p3_send,
     p3_recv,
-    l3_keep,
+    l3_rows,
     l3_recv,
     in_sem,
     par_send_sem,
@@ -153,24 +161,29 @@
         )
 
     messages = {
-        Z_RIGHT: lambda h: message(Z_RIGHT, h, kv.at[h, 2], kv.at[h, 0], at_right),
-        Z_LEFT: lambda h: message(Z_LEFT, h, kv.at[h, 1], kv.at[h, 3], at_left),
+        Z_RIGHT0: lambda h: message(Z_RIGHT0, h, kv0.at[h, 2], kv0.at[h, 0], at_right),
+        Z_LEFT0: lambda h: message(Z_LEFT0, h, kv0.at[h, 1], kv0.at[h, 3], at_left),
+        Z_RIGHT1: lambda h: message(Z_RIGHT1, h, kv1.at[h, 2], kv1.at[h, 0], at_right),
+        Z_LEFT1: lambda h: message(Z_LEFT1, h, kv1.at[h, 1], kv1.at[h, 3], at_left),
         Q_CHIP: lambda h: message(Q_CHIP, h, q.at[h, 0, O], q.at[h, 2, O], chip_mate),
         Q_UP: lambda h: message(Q_UP, h, q.at[h, 0, O], q.at[h, 2, D], at_up),
+        Q_UP2: lambda h: message(Q_UP2, h, q.at[h, 2, O], q.at[h, 0, D], at_up),
         Q_DOWN: lambda h: message(Q_DOWN, h, q.at[h, 0, O], q.at[h, 2, U], at_down),
-        Q_PASS: lambda h: message(
-            Q_PASS, h, q.at[h, 2, pl.ds(U, 2)], q.at[h, 0, pl.ds(U, 2)], chip_mate
-        ),
+        Q_PASS: lambda h: message(Q_PASS, h, q.at[h, 2, U], q.at[h, 0, U], chip_mate),
         Q_CORE0: lambda h: message(Q_CORE0, h, q.at[h, 0], q.at[h, 1], core_mate),
         Q_CORE2: lambda h: message(Q_CORE2, h, q.at[h, 2], q.at[h, 3], core_mate),
-        P_CORE: lambda h: message(P_CORE, h, p1_send.at[h], p1_recv.at[h], core_mate),
-        L_CORE: lambda h: message(L_CORE, h, l1_send.at[h], l1_recv.at[h], core_mate),
-        P_CHIP: lambda h: message(P_CHIP, h, p2_send.at[h], p2_recv.at[h], chip_mate),
-        L_CHIP: lambda h: message(L_CHIP, h, l2_send.at[h], l2_recv.at[h], chip_mate),
+        P_CORE0: lambda h: message(P_CORE0, h, p1_send.at[h, 0], p1_recv.at[h, 0], core_mate),
+        L_CORE0: lambda h: message(L_CORE0, h, l1_send.at[h, 0], l1_recv.at[h, 0], core_mate),
+        P_CORE1: lambda h: message(P_CORE1, h, p1_send.at[h, 1], p1_recv.at[h, 1], core_mate),
+        L_CORE1: lambda h: message(L_CORE1, h, l1_send.at[h, 1], l1_recv.at[h, 1], core_mate),
+        P_CHIP0: lambda h: message(P_CHIP0, h, p2_send0.at[h], p2_recv0.at[h], chip_mate),
+        L_CHIP0: lambda h: message(L_CHIP0, h, l2_rows.at[h, 0], l2_recv.at[h, 0], chip_mate),
+        P_CHIP1: lambda h: message(P_CHIP1, h, p2_send1.at[h], p2_recv1.at[h], chip_mate),
+        L_CHIP1: lambda h: message(L_CHIP1, h, l2_rows.at[h, 1], l2_recv.at[h, 1], chip_mate),
         P_UP: lambda h: message(P_UP, h, p3_send.at[h, 0], p3_recv.at[h, 0], at_up),
-        L_UP: lambda h: message(L_UP, h, l3_keep.at[h], l3_recv.at[h, 0], at_up),
+        L_UP: lambda h: message(L_UP, h, l3_rows.at[h], l3_recv.at[h, 0], at_up),
         P_DOWN: lambda h: message(P_DOWN, h, p3_send.at[h, 1], p3_recv.at[h, 1], at_down),
-        L_DOWN: lambda h: message(L_DOWN, h, l3_keep.at[h], l3_recv.at[h, 1], at_down),
+        L_DOWN: lambda h: message(L_DOWN, h, l3_rows.at[h], l3_recv.at[h, 1], at_down),
     }
 
     def start(h, *numbers):
@@ -229,7 +242,7 @@
             return chip_slot
         return 3 - slot
 
-    def prepare_block(h, e, keys, values, n):
+    def prepare_block(h, kv, e, keys, values, n):
         both = dot(quarters, jnp.concatenate([keys, values], axis=1))
         new_keys = turned(both[:, :HD], n).astype(jnp.bfloat16)
         new_values = both[:, HD:].astype(jnp.bfloat16)
@@ -242,9 +255,10 @@
     def prepare(h):
         for e in range(GROUPS):
             lanes = pl.ds(pl.multiple_of((group_of(e) * ROUNDS + h) * HD, HD), HD)
-            prepare_block(h, e, ck_in[0, 0, :, lanes], cv_in[0, 0, :, lanes], 0)
+            kv = kv0 if e < 2 else kv1
+            prepare_block(h, kv, e % 2, ck_in[0, 0, :, lanes], cv_in[0, 0, :, lanes], 0)
         lanes = pl.ds(pl.multiple_of(h * HD, HD), HD)
-        prepare_block(h, GROUPS, k_in[0, :, lanes], v_in[0, :, lanes], 1)
+        prepare_block(h, kv0, 2, k_in[0, :, lanes], v_in[0, :, lanes], 1)
         q[h, 0, O] = turned(q_in[0, :, lanes], 2).astype(jnp.bfloat16)
 
     entry = iota((16, HD), 0)
@@ -257,6 +271,7 @@
 
     for copy in inputs:
         copy.wait()
+    prepare(0)
     pl.semaphore_wait(barrier, len(partners))
 
     par_copies = [
@@ -273,12 +288,37 @@
     for copy in par_copies:
         copy.start()
 
+    def relay(h):
+        arrived(h, Q_CHIP)
+        start(h, Q_UP2)
+        arrived(h, Q_DOWN)
+        start(h, Q_PASS)
+
+    def share(h):
+        arrived(h, Q_UP)
+        start(h, Q_CORE2)
+        arrived(h, Q_PASS, Q_UP2)
+        start(h, Q_CORE0)
+
+    def ask(h):
+        start(h, Q_CHIP, Q_DOWN, Q_UP)
+
+    start(0, Z_RIGHT0, Z_LEFT0, Z_RIGHT1, Z_LEFT1)
+    ask(0)
+
     def first_sends(h, carry):
         prepare(h)
-        start(h, Z_RIGHT, Z_LEFT, Q_UP, Q_DOWN, Q_CHIP)
+        start(h, Z_RIGHT0, Z_LEFT0, Z_RIGHT1, Z_LEFT1)
+
+        @pl.when(h == 1)
+        def _():
+            ask(1)
+
         return carry
 
-    lax.fori_loop(0, ROUNDS, first_sends, 0)
+    lax.fori_loop(1, ROUNDS, first_sends, 0)
+    relay(0)
+    ask(2)
 
     for copy in par_copies:
         copy.wait_recv()
@@ -306,159 +346,182 @@
             feature == 0, other, jnp.where(feature == 1, own_window, 0.0)
         ).astype(jnp.bfloat16)
 
-    def pass_on(h):
-        arrived(h, Q_UP, Q_DOWN)
-        start(h, Q_PASS)
-
-    def share(h):
-        arrived(h, Q_CHIP)
-        start(h, Q_CORE2)
-        arrived(h, Q_PASS)
-        start(h, Q_CORE0)
-
-    def attend(queries, marker, keys, values):
-        scores = nt_dot(jnp.concatenate([queries, marker], axis=1), keys)
-        highest = jnp.max(scores, axis=1, keepdims=True)
-        weights = jnp.exp2((scores - highest) * SCALE).astype(jnp.bfloat16)
-        summed = dot(weights, values)
-        total = summed[:, HD:]
-        return summed[:, :HD] / total, highest * SCALE + jnp.log2(total)
-
-    def compute(h):
+    def compute(h, groups):
         other_marker = jnp.where(feature == 0, 1.0, 0.0).astype(jnp.bfloat16)
         own_marker = jnp.where(feature == 1, 1.0, 0.0).astype(jnp.bfloat16)
         ones = jnp.ones((TOKT, HD), jnp.bfloat16)
-        kept = jnp.zeros((TOKT, HD), jnp.float32)
-        sent = jnp.zeros((TOKT, HD), jnp.float32)
-        for e in range(GROUPS):
-            keys, values = [[], []], [[], []]
-            for block_at in (e,) if e > 0 else (0, GROUPS):
-                for lower_half in range(2):
-                    these_keys = kv[h, :, 0, block_at, lower_half].reshape(TOKT, HD)
-                    these_values = kv[h, :, 1, block_at, lower_half].reshape(TOKT, HD)
-                    keys[lower_half].append(
-                        jnp.concatenate([these_keys, bias[lower_half]], axis=1)
-                    )
-                    values[lower_half].append(jnp.concatenate([these_values, ones], axis=1))
-            for tile_kind, halves, marker in (
-                (U, (0,), other_marker),
-                (D, (1,), other_marker),
-                (O, (0, 1), own_marker),
+        markers = (
+            jnp.concatenate([other_marker, own_marker], axis=0),
+            jnp.concatenate([own_marker, other_marker], axis=0),
+        )
+        all_levels = []
+        for e in groups:
+            levels = jnp.zeros((TOKT, HD), jnp.float32)
+            kv = kv0 if e < 2 else kv1
+            blocks = (e % 2,) if e > 0 else (0, 2)
+            scores, highest = [], []
+            for half in range(2):
+                keys = jnp.concatenate(
+                    [
+                        jnp.concatenate(
+                            [kv[h, :, 0, n, half].reshape(TOKT, HD), bias[half]], axis=1
+                        )
+                        for n in blocks
+                    ],
+                    axis=0,
+                )
+                queries = q[h, e, pl.ds(half, 2)].reshape(2 * TOKT, HD)
+                found = nt_dot(jnp.concatenate([queries, markers[half]], axis=1), keys)
+                scores.append(found)
+                highest.append(jnp.max(found, axis=1, keepdims=True))
+            top, bottom = highest
+            own = jnp.maximum(top[TOKT:], bottom[:TOKT])
+            highest = (
+                jnp.concatenate([top[:TOKT], own], axis=0),
+                jnp.concatenate([own, bottom[TOKT:]], axis=0),
+            )
+            summed = []
+            for half in range(2):
+                weights = jnp.exp2((scores[half] - highest[half]) * SCALE).astype(jnp.bfloat16)
+                values = jnp.concatenate(
+                    [
+                        jnp.concatenate([kv[h, :, 1, n, half].reshape(TOKT, HD), ones], axis=1)
+                        for n in blocks
+                    ],
+                    axis=0,
+                )
+                summed.append(dot(weights, values))
+            for tile_kind, result, level in (
+                (U, summed[0][:TOKT], top[:TOKT]),
+                (O, summed[0][TOKT:] + summed[1][:TOKT], own),
+                (D, summed[1][TOKT:], bottom[TOKT:]),
             ):
-                all_keys = jnp.concatenate([x for n in halves for x in keys[n]], axis=0)
-                all_values = jnp.concatenate([x for n in halves for x in values[n]], axis=0)
-                result, level = attend(q[h, e, tile_kind], marker, all_keys, all_values)
-                place = e // 2 * 3 + tile_kind
+                total = result[:, HD:]
+                level = level * SCALE + jnp.log2(total)
+                result = result[:, :HD] / total
                 if e % 2 == 0:
                     part[e // 2, tile_kind] = result
-                    kept = jnp.where(feature == place, level, kept)
                 else:
                     p1_send[h, e // 2, tile_kind] = result.astype(jnp.bfloat16)
-                    sent = jnp.where(feature == place, level, sent)
-        lse[...] = kept
-        l1_send[h] = sent
-        start(h, P_CORE, L_CORE)
-
-    def after_core(h):
-        arrived(h, P_CORE, L_CORE)
-        mine, theirs = lse[...], l1_recv[h]
+                levels = jnp.where(feature == tile_kind, level, levels)
+            all_levels.append(levels)
+        return all_levels
+
+    def after_core(h, n):
+        arrived(h, *((P_CORE0, L_CORE0) if n == 0 else (P_CORE1, L_CORE1)))
+        mine, theirs = lse[n], l1_recv[h, n]
         newest = jnp.maximum(mine, theirs)
         mine_part, theirs_part = jnp.exp2(mine - newest), jnp.exp2(theirs - newest)
         total = mine_part + theirs_part
         mine_part, theirs_part = mine_part / total, theirs_part / total
-        rows = gathered(newest + jnp.log2(total))
         for tile_kind in range(3):
-            for n in range(2):
-                place = n * 3 + tile_kind
-                result = (
-                    part[n, tile_kind] * mine_part[:, place : place + 1]
-                    + p1_recv[h, n, tile_kind].astype(jnp.float32)
-                    * theirs_part[:, place : place + 1]
-                )
-                if (n == 0) == (tile_kind == O):
-                    p2_keep[h, tile_kind] = result
+            result = (
+                part[n, tile_kind] * mine_part[:, tile_kind : tile_kind + 1]
+                + p1_recv[h, n, tile_kind].astype(jnp.float32)
+                * theirs_part[:, tile_kind : tile_kind + 1]
+            )
+            if n == 0:
+                if tile_kind == O:
+                    keep0[h] = result
                 else:
-                    p2_send[h, tile_kind] = result.astype(jnp.bfloat16)
-        start(h, P_CHIP)
-        l2_keep[h] = rows
-        l2_send[h] = jnp.concatenate(
-            [rows[3:4], rows[0:1], rows[0:1], rows[0:1], rows[1:2], rows[2:3], rows[0:2]], axis=0
-        )
-        start(h, L_CHIP)
+                    p2_send0[h, tile_kind // 2] = result.astype(jnp.bfloat16)
+            elif tile_kind == O:
+                p2_send1[h] = result.astype(jnp.bfloat16)
+            else:
+                keep1[h, tile_kind // 2] = result
+        start(h, P_CHIP0 if n == 0 else P_CHIP1)
+        l2_rows[h, n] = gathered(newest + jnp.log2(total))
+        start(h, L_CHIP0 if n == 0 else L_CHIP1)
 
     def after_chip(h):
-        arrived(h, P_CHIP, L_CHIP)
-        mine, theirs = l2_keep[h], l2_recv[h]
+        arrived(h, P_CHIP0, L_CHIP0)
+        mine, theirs = l2_rows[h, 1], l2_recv[h, 0]
         newest = jnp.maximum(mine, theirs)
         mine_part, theirs_part = jnp.exp2(mine - newest), jnp.exp2(theirs - newest)
         total = mine_part + theirs_part
-        l3_keep[h] = newest + jnp.log2(total)
+        l3_rows[h] = newest + jnp.log2(total)
         start(h, L_UP, L_DOWN)
         columns = spread(jnp.concatenate([mine_part / total, theirs_part / total], axis=0))
-        for tile_kind, place in ((U, 4), (D, 5), (O, 0)):
+        for n, (tile_kind, number) in enumerate(((U, P_UP), (D, P_DOWN))):
             result = (
-                p2_keep[h, tile_kind] * columns[:, place : place + 1]
-                + p2_recv[h, tile_kind].astype(jnp.float32) * columns[:, 8 + place : 9 + place]
+                keep1[h, n] * columns[:, tile_kind : tile_kind + 1]
+                + p2_recv0[h, n].astype(jnp.float32) * columns[:, 8 + tile_kind : 9 + tile_kind]
             )
-            if tile_kind == O:
-                p3_keep[h] = result
-            else:
-                p3_send[h, tile_kind - 1] = result.astype(jnp.bfloat16)
-                start(h, P_UP if tile_kind == U else P_DOWN)
+            p3_send[h, n] = result.astype(jnp.bfloat16)
+            start(h, number)
 
     def after_row(h):
-        arrived(h, P_UP, L_UP, P_DOWN, L_DOWN)
-        own = l3_keep[h][0:1]
-        from_down = l3_recv[h, 0][4:5]
-        from_up = l3_recv[h, 1][5:6]
-        newest = jnp.maximum(jnp.maximum(own, from_down), from_up)
-        parts = [jnp.exp2(x - newest) for x in (own, from_down, from_up)]
-        total = parts[0] + parts[1] + parts[2]
+        arrived(h, P_CHIP1, L_CHIP1, P_UP, L_UP, P_DOWN, L_DOWN)
+        levels = (
+            l2_rows[h, 0][O : O + 1],
+            l2_recv[h, 1][O : O + 1],
+            l3_recv[h, 0][U : U + 1],
+            l3_recv[h, 1][D : D + 1],
+        )
+        newest = functools.reduce(jnp.maximum, levels)
+        parts = [jnp.exp2(x - newest) for x in levels]
+        total = parts[0] + parts[1] + parts[2] + parts[3]
         columns = spread(
             jnp.concatenate(
-                [x / total for x in parts] + [jnp.zeros((5, 256), jnp.float32)], axis=0
+                [x / total for x in parts] + [jnp.zeros((4, 256), jnp.float32)], axis=0
             )
         )
         result = (
-            p3_keep[h] * columns[:, 0:1]
-            + p3_recv[h, 0].astype(jnp.float32) * columns[:, 1:2]
-            + p3_recv[h, 1].astype(jnp.float32) * columns[:, 2:3]
+            keep0[h] * columns[:, 0:1]
+            + p2_recv1[h].astype(jnp.float32) * columns[:, 1:2]
+            + p3_recv[h, 0].astype(jnp.float32) * columns[:, 2:3]
+            + p3_recv[h, 1].astype(jnp.float32) * columns[:, 3:4]
         )
         lanes = pl.ds(pl.multiple_of(h * HD, HD), HD)
         out_ref[0, :, lanes] = result.astype(jnp.bfloat16)
 
-    pass_on(0)
     share(0)
+    relay(1)
+    ask(3)
 
     def step(i, carry):
-        @pl.when(i + 1 < ROUNDS)
+        arrived(i, Q_CORE0, Q_CORE2, Z_RIGHT0, Z_LEFT0, Z_RIGHT1, Z_LEFT1)
+        l1_send[i, 0], l1_send[i, 1], lse[0], lse[1] = compute(i, (1, 3, 0, 2))
+        start(i, P_CORE0, L_CORE0, P_CORE1, L_CORE1)
+        share(i + 1)
+
+        @pl.when(i + 2 < ROUNDS)
         def _():
-            pass_on(i + 1)
-
-        @pl.when((i >= 1) & (i <= ROUNDS))
+            relay(i + 2)
+
+        @pl.when(i + 4 < ROUNDS)
         def _():
-            after_core(i - 1)
-
-        @pl.when((i >= 2) & (i <= ROUNDS + 1))
+            ask(i + 4)
+
+        after_core(i, 0)
+        after_core(i, 1)
+
+        @pl.when(i >= 1)
         def _():
-            after_chip(i - 2)
-
-        @pl.when(i >= 3)
+            after_chip(i - 1)
+
+        @pl.when(i >= 2)
         def _():
-            after_row(i - 3)
-
-        @pl.when(i + 1 < ROUNDS)
-        def _():
-            share(i + 1)
-
-        @pl.when(i < ROUNDS)
-        def _():
-            arrived(i, Q_CORE0, Q_CORE2, Z_RIGHT, Z_LEFT)
-            compute(i)
+            after_row(i - 2)
 
         return carry
 
-    lax.fori_loop(0, ROUNDS + 3, step, 0)
+    lax.fori_loop(0, ROUNDS - 1, step, 0)
+
+    last = ROUNDS - 1
+    arrived(last, Q_CORE0, Q_CORE2, Z_RIGHT0, Z_LEFT0)
+    l1_send[last, 0], lse[0] = compute(last, (1, 0))
+    start(last, P_CORE0, L_CORE0)
+    after_core(last, 0)
+    arrived(last, Z_RIGHT1, Z_LEFT1)
+    l1_send[last, 1], lse[1] = compute(last, (3, 2))
+    start(last, P_CORE1, L_CORE1)
+    after_chip(last - 1)
+    after_core(last, 1)
+    after_chip(last)
+    after_row(last - 2)
+    after_row(last - 1)
+    after_row(last)
 
     def finish(h, carry):
         for number in range(MESSAGES):
@@ -490,7 +553,8 @@
                 pltpu.VMEM((1, TOKT, ROUNDS * HD), bf16),
                 pltpu.VMEM((1, 1, TOKT, wide), bf16),
                 pltpu.VMEM((1, 1, TOKT, wide), bf16),
-                pltpu.VMEM((ROUNDS, 4, 2, BLOCKS, 2, HALF, HD), bf16),
+                pltpu.VMEM((ROUNDS, 4, 2, 3, 2, HALF, HD), bf16),
+                pltpu.VMEM((ROUNDS, 4, 2, 2, 2, HALF, HD), bf16),
                 pltpu.VMEM((ROUNDS, GROUPS, 3) + piece, bf16),
                 pltpu.VMEM((16, HD), i32),
                 pltpu.VMEM((16, HD), i32),
@@ -498,18 +562,19 @@
                 pltpu.VMEM((2,) + piece, bf16),
                 pltpu.VMEM((3, 2) + piece, f32),
                 pltpu.VMEM((2, 3) + piece, f32),
-                pltpu.VMEM(piece, f32),
+                pltpu.VMEM((2,) + piece, f32),
                 pltpu.VMEM((ROUNDS, 2, 3) + piece, bf16),
                 pltpu.VMEM((ROUNDS, 2, 3) + piece, bf16),
+                pltpu.VMEM((ROUNDS, 2) + piece, f32),
+                pltpu.VMEM((ROUNDS, 2) + piece, f32),
+                pltpu.VMEM((ROUNDS, 2) + piece, bf16),
+                pltpu.VMEM((ROUNDS, 2) + piece, bf16),
+                pltpu.VMEM((ROUNDS,) + piece, bf16),
+                pltpu.VMEM((ROUNDS,) + piece, bf16),
                 pltpu.VMEM((ROUNDS,) + piece, f32),
-                pltpu.VMEM((ROUNDS,) + piece, f32),
-                pltpu.VMEM((ROUNDS, 3) + piece, f32),
-                pltpu.VMEM((ROUNDS, 3) + piece, bf16),
-                pltpu.VMEM((ROUNDS, 3) + piece, bf16),
-                pltpu.VMEM((ROUNDS, 8, 256), f32),
-                pltpu.VMEM((ROUNDS, 8, 256), f32),
-                pltpu.VMEM((ROUNDS, 8, 256), f32),
-                pltpu.VMEM((ROUNDS,) + piece, f32),
+                pltpu.VMEM((ROUNDS, 2) + piece, f32),
+                pltpu.VMEM((ROUNDS, 2, 8, 256), f32),
+                pltpu.VMEM((ROUNDS, 2, 8, 256), f32),
                 pltpu.VMEM((ROUNDS, 2) + piece, bf16),
                 pltpu.VMEM((ROUNDS, 2) + piece, bf16),
                 pltpu.VMEM((ROUNDS, 8, 256), f32),

time: 66.2 us -> 57.1 us (0.86); the launches traced: 65.1 us -> 57 us
  Pallas kernels: 63.4 us -> 55.3 us
    pallas_call x1, Pallas kernels: 63.4 us -> 55.3 us  [on_device(): pl.pallas_call(functools.partial(kernel, grid_rows), out_shape=jax.ShapeD...]
where the time goes in v2:
time: 57.1 us; the launch traced here: 57 us
  Pallas kernels  55.3 us (97%)
  local copies, waits for them, and re-layouts  1.66 us (3%)
    pallas_call x1, Pallas kernels, on_device(): pl.pallas_call(functools.partial(kernel, grid_rows), out_shape=jax.ShapeD...  55.3 us
    unnamed x1, local copies, waits for them, and re-layouts  1.66 us

profile of v2, /device:TPU:1, one launch (start us, length us, event | category | flops | bytes accessed | tf_op | source)
XLA Modules:
  0.0 57.0 jit_solution(5441075732051317689)
XLA Ops:
  0.0 55.3 %shard_map.82 = bf16[1,192,640]{2,1,0:T(8,128)(2,1)} custom-call(s32[4]{0:T(128)} %order_ref.1, s32[1,9]{1,0:T(1,128)} %mask_ref.1, s32[1,2]{1,0:T(1,128)} %reach_ref.1, bf16[1,192,640]{2,1,0:T(8,128)(2,1)} %q_hbm.1, bf16[1,192,640]{2,1,0:T(8,128)(2,1)} %k_hbm.1, bf16[1,192,640]{2,1,0:T(8,128)(2,1)} %v_hbm.1, bf16[1,1,192,2560]{3,2,1,0:T(8,128)(2,1)} %ck_hbm.1, ...), custom_call_target="tpu_custom_call" | custom-call | tf_op jit(solution)/shard_map/pallas_call | solution.py:545
  55.3 1.7 %copy.10 = bf16[1,192,640]{2,1,0:T(8,128)(2,1)} copy(bf16[1,192,640]{2,1,0:T(8,128)(2,1)} %shard_map.82) | data formatting | bytes 491520

commit v3 on v2

--- a/solution.py
+++ b/solution.py
@@ -350,6 +350,9 @@
         other_marker = jnp.where(feature == 0, 1.0, 0.0).astype(jnp.bfloat16)
         own_marker = jnp.where(feature == 1, 1.0, 0.0).astype(jnp.bfloat16)
         ones = jnp.ones((TOKT, HD), jnp.bfloat16)
+        nothing = jnp.concatenate(
+            [jnp.zeros((64, HD), jnp.bfloat16), jnp.full((64, HD), NEGATIVE, jnp.bfloat16)], axis=1
+        )
         markers = (
             jnp.concatenate([other_marker, own_marker], axis=0),
             jnp.concatenate([own_marker, other_marker], axis=0),
@@ -367,7 +370,8 @@
                             [kv[h, :, 0, n, half].reshape(TOKT, HD), bias[half]], axis=1
                         )
                         for n in blocks
-                    ],
+                    ]
+                    + ([nothing] if len(blocks) == 1 else []),
                     axis=0,
                 )
                 queries = q[h, e, pl.ds(half, 2)].reshape(2 * TOKT, HD)
@@ -382,12 +386,13 @@
             )
             summed = []
             for half in range(2):
-                weights = jnp.exp2((scores[half] - highest[half]) * SCALE).astype(jnp.bfloat16)
+                weights = jnp.exp2(scores[half] * SCALE - highest[half] * SCALE).astype(jnp.bfloat16)
                 values = jnp.concatenate(
                     [
                         jnp.concatenate([kv[h, :, 1, n, half].reshape(TOKT, HD), ones], axis=1)
                         for n in blocks
-                    ],
+                    ]
+                    + ([jnp.zeros((64, 2 * HD), jnp.bfloat16)] if len(blocks) == 1 else []),
                     axis=0,
                 )
                 summed.append(dot(weights, values))
@@ -480,48 +485,41 @@
     ask(3)
 
     def step(i, carry):
-        arrived(i, Q_CORE0, Q_CORE2, Z_RIGHT0, Z_LEFT0, Z_RIGHT1, Z_LEFT1)
-        l1_send[i, 0], l1_send[i, 1], lse[0], lse[1] = compute(i, (1, 3, 0, 2))
-        start(i, P_CORE0, L_CORE0, P_CORE1, L_CORE1)
-        share(i + 1)
-
-        @pl.when(i + 2 < ROUNDS)
+        @pl.when(i < ROUNDS)
         def _():
-            relay(i + 2)
-
-        @pl.when(i + 4 < ROUNDS)
-        def _():
-            ask(i + 4)
-
-        after_core(i, 0)
-        after_core(i, 1)
+            arrived(i, Q_CORE0, Q_CORE2, Z_RIGHT0, Z_LEFT0, Z_RIGHT1, Z_LEFT1)
+            l1_send[i, 0], l1_send[i, 1] = compute(i, (1, 3))
+            start(i, P_CORE0, L_CORE0, P_CORE1, L_CORE1)
+            lse[0], lse[1] = compute(i, (0, 2))
+
+            @pl.when(i + 1 < ROUNDS)
+            def _():
+                share(i + 1)
+
+            @pl.when(i + 2 < ROUNDS)
+            def _():
+                relay(i + 2)
+
+            @pl.when(i + 4 < ROUNDS)
+            def _():
+                ask(i + 4)
+
+            after_core(i, 0)
+            after_core(i, 1)
 
         @pl.when(i >= 1)
         def _():
             after_chip(i - 1)
 
-        @pl.when(i >= 2)
-        def _():
-            after_row(i - 2)
-
         return carry
 
-    lax.fori_loop(0, ROUNDS - 1, step, 0)
-
-    last = ROUNDS - 1
-    arrived(last, Q_CORE0, Q_CORE2, Z_RIGHT0, Z_LEFT0)
-    l1_send[last, 0], lse[0] = compute(last, (1, 0))
-    start(last, P_CORE0, L_CORE0)
-    after_core(last, 0)
-    arrived(last, Z_RIGHT1, Z_LEFT1)
-    l1_send[last, 1], lse[1] = compute(last, (3, 2))
-    start(last, P_CORE1, L_CORE1)
-    after_chip(last - 1)
-    after_core(last, 1)
-    after_chip(last)
-    after_row(last - 2)
-    after_row(last - 1)
-    after_row(last)
+    lax.fori_loop(0, ROUNDS + 1, step, 0)
+
+    def result_of(h, carry):
+        after_row(h)
+        return carry
+
+    lax.fori_loop(0, ROUNDS, result_of, 0)
 
     def finish(h, carry):
         for number in range(MESSAGES):

time: 57.1 us -> 55.5 us (0.972)
  Pallas kernels: 55.3 us -> 53.7 us
    pallas_call x1, Pallas kernels: 55.3 us -> 53.7 us  [on_device(): pl.pallas_call(functools.partial(kernel, grid_rows), out_shape=jax.ShapeD...]
where the time goes in v3:
time: 55.5 us; the launch traced here: 55.3 us
  Pallas kernels  53.7 us (97%)
  local copies, waits for them, and re-layouts  1.66 us (3%)
    pallas_call x1, Pallas kernels, on_device(): pl.pallas_call(functools.partial(kernel, grid_rows), out_shape=jax.ShapeD...  53.7 us
    unnamed x1, local copies, waits for them, and re-layouts  1.66 us

profile of v3, /device:TPU:1, one launch (start us, length us, event | category | flops | bytes accessed | tf_op | source)
XLA Modules:
  0.0 55.3 jit_solution(14247681755661503669)
XLA Ops:
  0.0 53.7 %shard_map.82 = bf16[1,192,640]{2,1,0:T(8,128)(2,1)} custom-call(s32[4]{0:T(128)} %order_ref.1, s32[1,9]{1,0:T(1,128)} %mask_ref.1, s32[1,2]{1,0:T(1,128)} %reach_ref.1, bf16[1,192,640]{2,1,0:T(8,128)(2,1)} %q_hbm.1, bf16[1,192,640]{2,1,0:T(8,128)(2,1)} %k_hbm.1, bf16[1,192,640]{2,1,0:T(8,128)(2,1)} %v_hbm.1, bf16[1,1,192,2560]{3,2,1,0:T(8,128)(2,1)} %ck_hbm.1, ...), custom_call_target="tpu_custom_call" | custom-call | tf_op jit(solution)/shard_map/pallas_call | solution.py:543
  53.7 1.7 %copy.10 = bf16[1,192,640]{2,1,0:T(8,128)(2,1)} copy(bf16[1,192,640]{2,1,0:T(8,128)(2,1)} %shard_map.82) | data formatting | bytes 491520

commit v4 on v3

--- a/solution.py
+++ b/solution.py
@@ -419,7 +419,7 @@
         mine_part, theirs_part = jnp.exp2(mine - newest), jnp.exp2(theirs - newest)
         total = mine_part + theirs_part
         mine_part, theirs_part = mine_part / total, theirs_part / total
-        for tile_kind in range(3):
+        for tile_kind in (U, D, O) if n == 0 else (O, U, D):
             result = (
                 part[n, tile_kind] * mine_part[:, tile_kind : tile_kind + 1]
                 + p1_recv[h, n, tile_kind].astype(jnp.float32)
@@ -434,7 +434,8 @@
                 p2_send1[h] = result.astype(jnp.bfloat16)
             else:
                 keep1[h, tile_kind // 2] = result
-        start(h, P_CHIP0 if n == 0 else P_CHIP1)
+            if tile_kind == (D if n == 0 else O):
+                start(h, P_CHIP0 if n == 0 else P_CHIP1)
         l2_rows[h, n] = gathered(newest + jnp.log2(total))
         start(h, L_CHIP0 if n == 0 else L_CHIP1)
 

time: 55.5 us -> 55.4 us (level)
  no operation moved by 1% of the time
where the time goes in v4:
time: 55.4 us; the launch traced here: 55.3 us
  Pallas kernels  53.6 us (97%)
  local copies, waits for them, and re-layouts  1.66 us (3%)
    pallas_call x1, Pallas kernels, on_device(): pl.pallas_call(functools.partial(kernel, grid_rows), out_shape=jax.ShapeD...  53.6 us
    unnamed x1, local copies, waits for them, and re-layouts  1.66 us

profile of v4, /device:TPU:1, one launch (start us, length us, event | category | flops | bytes accessed | tf_op | source)
XLA Modules:
  0.0 55.3 jit_solution(11872021917538019426)
XLA Ops:
  0.0 53.6 %shard_map.82 = bf16[1,192,640]{2,1,0:T(8,128)(2,1)} custom-call(s32[4]{0:T(128)} %order_ref.1, s32[1,9]{1,0:T(1,128)} %mask_ref.1, s32[1,2]{1,0:T(1,128)} %reach_ref.1, bf16[1,192,640]{2,1,0:T(8,128)(2,1)} %q_hbm.1, bf16[1,192,640]{2,1,0:T(8,128)(2,1)} %k_hbm.1, bf16[1,192,640]{2,1,0:T(8,128)(2,1)} %v_hbm.1, bf16[1,1,192,2560]{3,2,1,0:T(8,128)(2,1)} %ck_hbm.1, ...), custom_call_target="tpu_custom_call" | custom-call | tf_op jit(solution)/shard_map/pallas_call | solution.py:544
  53.6 1.7 %copy.10 = bf16[1,192,640]{2,1,0:T(8,128)(2,1)} copy(bf16[1,192,640]{2,1,0:T(8,128)(2,1)} %shard_map.82) | data formatting | bytes 491520
